TPU v7x, 256 devices: a whole 4x4x8 slice. The times are simulated.
256 devices in a mesh: gx: 16 (over y, x), gy: 2 (over core), gz: 8 (over z).
Axes of the slice: x: 4, y: 4, z: 8, core: 2. Of those that a mesh axis runs over, the one named last changes fastest.
Arguments:
- fields: float32 [8, 128, 256, 256], P(None, 'gz', 'gx', 'gy'), as said below
- col_cells: int32 [128], replicated, may hold values from 0 to 255, as said below
- col_num: int32 [128], replicated, may hold values from 0 to 63
- shear_sub: int32 [1], replicated, may hold values from 0 to 16383
Outputs:
- updated: float32 [8, 128, 256, 256], P(None, 'gz', 'gx', 'gy')
Inputs may be any that keep to these rules, and one draw needn't show every extreme that they name: `col_cells`: the whole-cell shifts run over the whole azimuthal loop. The density fields[0] lies between 0.5 and 2.
All inputs are finite; a program needn't handle non-finite values.
Results may differ from a plain program's by a relative error of at most 0.0003.
Values sent between devices are 32-bit elements; how exact they have to be, the bound alone decides.
No kernel may reach another device: no remote copies, remote signals or barrier semaphores. Data moves between devices by JAX's collectives and lax.ppermute only.
A program may use at most 128 MiB of HBM per device.

v0:
```python
import jax
import jax.numpy as jnp
from jax import lax
from jax.sharding import PartitionSpec as P

DEN = 64


time_step = 0.2
gravity_rate = 4.0


def with_halo(block, sides, width):
    for axis, dim in sides:
        count = lax.axis_size(axis)
        forward = [(i, i + 1) for i in range(count - 1)]
        forward.append((count - 1, 0))
        backward = [(target, source) for source, target in forward]
        low = lax.ppermute(
            lax.slice_in_dim(block, block.shape[dim] - width, None, axis=dim), axis, forward
        )
        high = lax.ppermute(lax.slice_in_dim(block, 0, width, axis=dim), axis, backward)
        block = jnp.concatenate([low, block, high], axis=dim)
    return block


def minmod(left, right):
    return 0.5 * (jnp.sign(left) + jnp.sign(right)) * jnp.minimum(jnp.abs(left), jnp.abs(right))


def divergence(values, speed, axis):
    length = values.shape[axis] - 4
    minus = lax.slice_in_dim(values, 1, length + 3, axis=axis) - lax.slice_in_dim(
        values, 0, length + 2, axis=axis
    )
    plus = lax.slice_in_dim(values, 2, length + 4, axis=axis) - lax.slice_in_dim(
        values, 1, length + 3, axis=axis
    )
    slope = minmod(minus, plus)
    left_state = lax.slice_in_dim(values, 1, length + 2, axis=axis) + 0.5 * lax.slice_in_dim(
        slope, 0, length + 1, axis=axis
    )
    right_state = lax.slice_in_dim(values, 2, length + 3, axis=axis) - 0.5 * lax.slice_in_dim(
        slope, 1, length + 2, axis=axis
    )
    face_speed = 0.5 * (
        lax.slice_in_dim(speed, 1, length + 2, axis=axis - 1)
        + lax.slice_in_dim(speed, 2, length + 3, axis=axis - 1)
    )
    face_speed = jnp.expand_dims(face_speed, 0)
    flux = jnp.maximum(face_speed, 0.0) * left_state + jnp.minimum(face_speed, 0.0) * right_state
    return lax.slice_in_dim(flux, 1, length + 1, axis=axis) - lax.slice_in_dim(
        flux, 0, length, axis=axis
    )


def tendency(padded):
    density = padded[0]
    div_x = divergence(padded[:, :, 2:-2, 2:-2], (padded[1] / density)[:, 2:-2, 2:-2], 1)
    div_y = divergence(padded[:, 2:-2, :, 2:-2], (padded[2] / density)[2:-2, :, 2:-2], 2)
    div_z = divergence(padded[:, 2:-2, 2:-2, :], (padded[3] / density)[2:-2, 2:-2, :], 3)
    return div_x + div_y + div_z


def local(fields, col_cells, col_num, shear_sub):
    comps, cx, cy, cz = fields.shape
    nx = cx * lax.axis_size("gz")
    ny = cy * lax.axis_size("gx")
    nz = cz * lax.axis_size("gy")
    xstart = lax.axis_index("gz") * cx
    ystart = lax.axis_index("gx") * cy
    zindex = lax.axis_index("gy")
    extended = with_halo(fields, (("gz", 1),), 2)
    tripled_cells = jnp.concatenate([col_cells, col_cells, col_cells])
    tripled_num = jnp.concatenate([col_num, col_num, col_num])
    offset = nx + xstart - 2
    cells_here = lax.dynamic_slice_in_dim(tripled_cells, offset, cx + 4)
    num_here = lax.dynamic_slice_in_dim(tripled_num, offset, cx + 4)
    global_x = xstart - 2 + jnp.arange(cx + 4, dtype=jnp.int32)
    shear = shear_sub[0]
    total = (
        DEN * cells_here
        + num_here
        + jnp.where(global_x < 0, shear, 0)
        - jnp.where(global_x >= nx, shear, 0)
    )
    shift_cells = total // DEN % ny
    frac = (total % DEN).astype(jnp.float32) / DEN
    targets = ystart + jnp.arange(cy, dtype=jnp.int32)
    first = (targets[None, :] - shift_cells[:, None]) % ny
    second = (first - 1) % ny
    piece = lax.all_gather(extended, "gx", axis=2, tiled=True)
    count = piece.shape[2]
    near_in = (first >= 0) & (first < count)
    near_val = jnp.take_along_axis(piece, jnp.clip(first, 0, count - 1)[None, :, :, None], axis=2)
    near_weight = jnp.where(near_in, (1.0 - frac)[:, None], 0.0)
    far_in = (second >= 0) & (second < count)
    far_val = jnp.take_along_axis(piece, jnp.clip(second, 0, count - 1)[None, :, :, None], axis=2)
    far_weight = jnp.where(far_in, frac[:, None], 0.0)
    remapped = near_weight[None, :, :, None] * near_val + far_weight[None, :, :, None] * far_val
    padded = with_halo(remapped, (("gx", 2), ("gy", 3)), 2)
    depth = jnp.arange(cz + 4, dtype=jnp.int32)
    bottom = (zindex == 0) & (depth < 2)
    top = (zindex == lax.axis_size("gy") - 1) & (depth >= cz + 2)
    padded = jnp.where(bottom[None, None, None, :], padded[:, :, :, 2:3], padded)
    padded = jnp.where(top[None, None, None, :], padded[:, :, :, cz + 1 : cz + 2], padded)
    interior = remapped[:, 2:-2]
    updated = interior - time_step * tendency(padded)
    layers = zindex * cz + jnp.arange(cz, dtype=jnp.int32)
    height = gravity_rate * ((layers.astype(jnp.float32) + 0.5) / nz - 0.5)
    updated = updated.at[3].add(-time_step * height[None, None, :] * interior[0])
    return updated


def solution(mesh):
    return jax.shard_map(
        local,
        mesh=mesh,
        in_specs=(P(None, "gz", "gx", "gy"), P(), P(), P()),
        out_specs=P(None, "gz", "gx", "gy"),
        check_vma=False,
    )
```

profile of v0, /device:TPU:1, one launch (start us, length us, event | category | flops | bytes accessed | tf_op | source)
XLA Modules:
  0.0 243.2 jit_solution(4632591600442977067)
XLA Ops:
  6.5 1.8 copy.89
  8.4 6.5 %collective-permute-start.1 = (f32[8,2,16,128]{3,0,2,1:T(8,128)S(1)}, f32[8,2,16,128]{3,0,2,1:T(8,128)S(1)}, u32[]{:S(2)}, u32[]{:S(2)}) collective-permute-start(f32[8,2,16,128]{3,0,2,1:T(8,128)S(1)} %get-tuple-element.29), channel_id=1, source_target_pairs={{1,0},{2,1},{3,2},{4,3},{5,4},{6,5},{7,6},{0,7},{9,8},{10,9},{11,1... | collective-permute-start | bytes 393224 | tf_op jit(solution)/shard_map/ppermute | solution.py:22
  14.9 2.2 collective-permute-done.1
  17.0 2.9 %collective-permute-done = f32[8,2,16,128]{3,0,2,1:T(8,128)S(1)} collective-permute-done((f32[8,2,16,128]{3,0,2,1:T(8,128)S(1)}, f32[8,2,16,128]{3,0,2,1:T(8,128)S(1)}, u32[]{:S(2)}, u32[]{:S(2)}) %collective-permute-start) | collective-permute-done | bytes 131104 | tf_op jit(solution)/shard_map/ppermute | solution.py:19
  19.9 1.2 pad_maximum_fusion.1
  21.9 0.1 broadcast_subtract_fusion
  22.0 0.1 bitcast_or_fusion.1
  22.3 0.1 and_bitcast_fusion.1
  22.4 0.1 and_select_fusion.1
  22.5 135.5 %all-gather.2.cloned.1.call-done = f32[8,20,256,128]{3,0,2,1:T(8,128)} async-done(((f32[8,20,16,128]{3,0,2,1:T(8,128)}), f32[8,20,256,128]{3,0,2,1:T(8,128)}) %all-gather.2.cloned.1.call-update) | async-done | bytes 20971536 | tf_op jit(solution)/shard_map/all_gather | solution.py:92
  158.0 10.9 %gather_fusion.1 = f32[320,8,128]{2,1,0:T(8,128)} fusion(f32[8,20,256,128]{3,0,2,1:T(8,128)} %all-gather.2.cloned.1.call-done, s32[320]{0:T(512)S(1)} %reshape.377), kind=kCustom, calls=%fused_computation.1.clone | custom fusion | bytes 2624000 | tf_op jit(solution)/shard_map/jit(take_along_axis)/gather | solution.py:98
  168.9 1.6 copy.93
  170.5 10.9 %gather_fusion = f32[320,8,128]{2,1,0:T(8,128)} fusion(f32[8,20,256,128]{3,0,2,1:T(8,128)} %all-gather.2.cloned.1.call-done, s32[320]{0:T(512)S(1)} %reshape.372), kind=kCustom, calls=%fused_computation.clone | custom fusion | bytes 2624000 | tf_op jit(solution)/shard_map/jit(take_along_axis)/gather | solution.py:95
  181.3 1.6 copy.92
  182.9 0.3 fusion.10
  183.2 0.1 fusion.41
  183.4 2.8 %collective-permute-start.3 = (f32[8,20,2,128]{3,0,2,1:T(8,128)S(1)}, f32[8,20,2,128]{3,0,2,1:T(8,128)S(1)}, u32[]{:S(2)}, u32[]{:S(2)}) collective-permute-start(f32[8,20,2,128]{3,0,2,1:T(8,128)S(1)} %copy.95), channel_id=1, source_target_pairs={{16,0},{32,16},{48,32},{64,48},{80,64},{96,80},{112,96},{128,112},... | collective-permute-start | bytes 491528 | tf_op jit(solution)/shard_map/ppermute | solution.py:22
  186.3 0.1 collective-permute-start.2
  186.4 2.7 %collective-permute-done.3 = f32[8,20,2,128]{3,0,2,1:T(8,128)S(1)} collective-permute-done((f32[8,20,2,128]{3,0,2,1:T(8,128)S(1)}, f32[8,20,2,128]{3,0,2,1:T(8,128)S(1)}, u32[]{:S(2)}, u32[]{:S(2)}) %collective-permute-start.3) | collective-permute-done | bytes 163872 | tf_op jit(solution)/shard_map/ppermute | solution.py:22
  189.1 0.1 copy.97
  189.2 5.2 %collective-permute-done.2 = f32[8,20,2,128]{3,0,2,1:T(8,128)S(1)} collective-permute-done((f32[8,20,2,128]{3,0,2,1:T(8,128)S(1)}, f32[8,20,2,128]{3,0,2,1:T(8,128)S(1)}, u32[]{:S(2)}, u32[]{:S(2)}) %collective-permute-start.2) | collective-permute-done | bytes 163872 | tf_op jit(solution)/shard_map/ppermute | solution.py:19
  194.4 0.1 copy.96
  194.5 0.7 copy-done.1
  195.2 0.3 pad_maximum_fusion
  195.5 2.5 %fusion.40 = (f32[8,20,20,2]{3,2,1,0:T(8,128)}, f32[8,20,20,2]{3,2,1,0:T(8,128)}) fusion(f32[8,20,20,128]{3,2,1,0:T(8,128)S(1)} %pad_maximum_fusion), kind=kLoop, calls=%fused_computation.119 | loop fusion | bytes 102400 | tf_op jit(solution)/shard_map/slice | solution.py:20
  198.0 3.2 %copy.101 = f32[8,20,20,2]{2,0,3,1:T(8,128)} copy(f32[8,20,20,2]{3,2,1,0:T(8,128)} %get-tuple-element.25) | data formatting | bytes 51200 | tf_op jit(solution)/shard_map/slice | solution.py:22
  201.2 1.9 collective-permute-start.5
  203.1 3.2 %copy.100 = f32[8,20,20,2]{2,0,3,1:T(8,128)} copy(f32[8,20,20,2]{3,2,1,0:T(8,128)} %get-tuple-element.24) | data formatting | bytes 51200 | tf_op jit(solution)/shard_map/slice | solution.py:20
  206.3 1.2 copy.110
  207.6 2.0 copy.103
  209.6 3.3 %copy.102 = f32[8,20,20,2]{3,2,1,0:T(8,128)} copy(f32[8,20,20,2]{2,0,3,1:T(8,128)} %collective-permute-done.4) | data formatting | bytes 51200 | tf_op jit(solution)/shard_map/ppermute | solution.py:19
  212.8 5.0 %maximum_select_fusion = f32[8,20,20,132]{3,2,1,0:T(8,128)S(1)} fusion(f32[8,20,20,2]{3,2,1,0:T(8,128)S(1)} %copy.103, f32[8,20,2,128]{3,2,1,0:T(2,128)S(1)} %copy.97, f32[8,20,16,128]{3,2,1,0:T(8,128)S(1)} %fusion.10, f32[8,20,2,128]{3,2,1,0:T(2,128)} %copy-done.1, f32[8,20,20,2]{3,2,1,0:T(8,128)} %copy.102, f32[8,20,20]{2,1,0:T(8,128)S(1)} %bitcast.38, ...), kind=kLoop, calls=%fused_computation.2 | loop fusion | flops 2112000 | bytes 3392132 | tf_op jit(solution)/shard_map/jit(_where)/select_n | solution.py:105
  217.8 1.9 copy-done
  219.7 0.6 slice.259
  220.3 1.2 copy.111
  221.5 2.7 %broadcast_select_fusion = f32[8,20,20,132]{3,2,1,0:T(8,128)S(1)} fusion(f32[8,20,20,132]{3,2,1,0:T(8,128)} %copy-done, f32[8,20,20]{2,1,0:T(8,128)S(1)} %bitcast.39, pred[132]{0:T(512)(128)(4,1)S(1)} %compare_and_fusion.1), kind=kLoop, calls=%fused_computation.14 | loop fusion | flops 422400 | bytes 3392132 | tf_op jit(solution)/shard_map/jit(_where)/select_n | solution.py:106
  224.2 1.9 minimum_multiply_fusion
  226.1 0.1 fusion.22
  226.3 1.7 minimum_multiply_fusion.1
  228.0 1.2 minimum_multiply_fusion.2
  229.2 0.2 broadcast_maximum_fusion
  229.4 0.2 fusion.43
  229.8 0.1 broadcast_maximum_fusion.2
  229.9 1.7 fusion.2
  231.6 1.0 fusion.7
  232.6 0.7 fusion.13
  233.3 1.5 fusion.18
  234.8 1.6 fusion.27
  (26 shorter events, 0.5 us)
Async XLA Ops:
  6.5 151.5 %all-gather.2.cloned.1.call-start = ((), (), s32[]{:S(2)}) async-start(), calls=%async_computation | async-start | bytes 22282240 | tf_op jit(solution)/shard_map/all_gather | solution.py:92
  8.4 8.6 %collective-permute-start.1 = (f32[8,2,16,128]{3,0,2,1:T(8,128)S(1)}, f32[8,2,16,128]{3,0,2,1:T(8,128)S(1)}, u32[]{:S(2)}, u32[]{:S(2)}) collective-permute-start(f32[8,2,16,128]{3,0,2,1:T(8,128)S(1)} %get-tuple-element.29), channel_id=1, source_target_pairs={{1,0},{2,1},{3,2},{4,3},{5,4},{6,5},{7,6},{0,7},{9,8},{10,9},{11,1... | collective-permute-start | bytes 393224 | tf_op jit(solution)/shard_map/ppermute | solution.py:22
  14.9 7.0 %copy-start.2 = (s32[128]{0:T(128)S(1)}, s32[128]{0:T(128)}, u32[]{:S(2)}) copy-start(s32[128]{0:T(128)} %param.9) | copy-start | bytes 1540
  14.9 7.0 %copy-start.3 = (s32[128]{0:T(128)S(1)}, s32[128]{0:T(128)}, u32[]{:S(2)}) copy-start(s32[128]{0:T(128)} %param.10) | copy-start | bytes 1540
  14.9 5.0 %collective-permute-start = (f32[8,2,16,128]{3,0,2,1:T(8,128)S(1)}, f32[8,2,16,128]{3,0,2,1:T(8,128)S(1)}, u32[]{:S(2)}, u32[]{:S(2)}) collective-permute-start(f32[8,2,16,128]{3,0,2,1:T(8,128)S(1)} %get-tuple-element.28), channel_id=1, source_target_pairs={{0,1},{1,2},{2,3},{3,4},{4,5},{5,6},{6,7},{7,0},{8,9},{9,10},{10,1... | collective-permute-start | bytes 393224 | tf_op jit(solution)/shard_map/ppermute | solution.py:19
  183.4 5.7 %collective-permute-start.3 = (f32[8,20,2,128]{3,0,2,1:T(8,128)S(1)}, f32[8,20,2,128]{3,0,2,1:T(8,128)S(1)}, u32[]{:S(2)}, u32[]{:S(2)}) collective-permute-start(f32[8,20,2,128]{3,0,2,1:T(8,128)S(1)} %copy.95), channel_id=1, source_target_pairs={{16,0},{32,16},{48,32},{64,48},{80,64},{96,80},{112,96},{128,112},... | collective-permute-start | bytes 491528 | tf_op jit(solution)/shard_map/ppermute | solution.py:22
  186.3 8.1 %collective-permute-start.2 = (f32[8,20,2,128]{3,0,2,1:T(8,128)S(1)}, f32[8,20,2,128]{3,0,2,1:T(8,128)S(1)}, u32[]{:S(2)}, u32[]{:S(2)}) collective-permute-start(f32[8,20,2,128]{3,0,2,1:T(8,128)S(1)} %copy.94), channel_id=1, source_target_pairs={{0,16},{16,32},{32,48},{48,64},{64,80},{80,96},{96,112},{112,128},... | collective-permute-start | bytes 491528 | tf_op jit(solution)/shard_map/ppermute | solution.py:19
  194.5 0.7 copy-start.1
  201.2 6.3 %collective-permute-start.5 = (f32[8,20,20,2]{2,0,3,1:T(8,128)}, f32[8,20,20,2]{2,0,3,1:T(8,128)}, u32[]{:S(2)}, u32[]{:S(2)}) collective-permute-start(f32[8,20,20,2]{2,0,3,1:T(8,128)} %copy.101), channel_id=1, source_target_pairs={{8,0},{0,8},{9,1},{1,9},{10,2},{2,10},{11,3},{3,11},{12,4},{4,12},... | collective-permute-start | bytes 76808 | tf_op jit(solution)/shard_map/ppermute | solution.py:22
  206.3 3.3 %collective-permute-start.4 = (f32[8,20,20,2]{2,0,3,1:T(8,128)}, f32[8,20,20,2]{2,0,3,1:T(8,128)}, u32[]{:S(2)}, u32[]{:S(2)}) collective-permute-start(f32[8,20,20,2]{2,0,3,1:T(8,128)} %copy.100), channel_id=1, source_target_pairs={{0,8},{8,0},{1,9},{9,1},{2,10},{10,2},{3,11},{11,3},{4,12},{12,4},... | collective-permute-start | bytes 76808 | tf_op jit(solution)/shard_map/ppermute | solution.py:19
  217.8 1.9 copy-start
Sparse Core Ops, SparseCore 0:
  21.3 136.6 all-gather.1
where the time goes:
time: 244 us; the launch traced here: 243 us
  waiting for transfers between devices  149 us (61%)
  local copies, waits for them, and re-layouts  47.3 us (19%)
  other arithmetic  21.8 us (9%)
  between operations  14.3 us (6%)
  starting transfers between devices  11.2 us (5%)
    all_gather x1, waiting for transfers between devices, local(): piece = lax.all_gather(extended, 'gx', axis=2, tiled=True)  136 us
    gather x3, local copies, waits for them, and re-layouts, local(): jnp.take_along_axis(piece, jnp.clip(first, 0, count - 1)[None, :, :, None...  12.5 us
    gather x3, local copies, waits for them, and re-layouts, local(): jnp.take_along_axis(piece, jnp.clip(second, 0, count - 1)[None, :, :, Non...  12.5 us
    ppermute x3, starting transfers between devices, with_halo(): lax.ppermute(lax.slice_in_dim(block, 0, width, axis=dim), axis, backward)  11.2 us
    ppermute x3, waiting for transfers between devices, with_halo(): lax.ppermute(lax.slice_in_dim(block, block.shape[dim] - width, None, axis...  8.1 us
    slice x5, local copies, waits for them, and re-layouts, with_halo(): lax.slice_in_dim(block, block.shape[dim] - width, None, axis=dim)  5.89 us
    select_n x1, other arithmetic, local(): jnp.where(bottom[None, None, None, :], padded[:, :, :, 2:3], padded)  4.97 us
  transfers between devices with their start and end apart: 7, of which 5 were waited for; matrix products, arithmetic and copies ran while one was open for 3% of the time, Pallas kernels for 0%

commit v1 on v0

v1 whole, which is shorter than its diff:
```python
import jax
import jax.numpy as jnp
from jax import lax
from jax.experimental import pallas as pl
from jax.experimental.pallas import tpu as pltpu
from jax.sharding import PartitionSpec as P

DT = 0.2
GRAVITY = 4.0
NZ = 256
NB = 16
VMEM = pl.BlockSpec(memory_space=pltpu.VMEM)
SMEM = pl.BlockSpec(memory_space=pltpu.SMEM)


def shift_kernel(cells_ref, num_ref, shear_ref, src_ref, out_ref, line):
    gz = lax.axis_index("gz")
    last = lax.axis_size("gz") - 1
    half = lax.rem(lax.axis_index("gx"), 2)
    first_col = gz * 16 + half * 8
    shear = shear_ref[0]
    side = jnp.where(
        half == 1, jnp.where(gz == last, shear, 0), jnp.where(gz == 0, -shear, 0)
    )

    def one(col, extra, row):
        total = 64 * cells_ref[first_col + col] + num_ref[first_col + col] + extra
        cells = (total >> 6) & 255
        frac = (total & 63).astype(jnp.float32) * (1.0 / 64.0)
        line[0:8] = src_ref[15, col, 8:16]
        for b in range(16):
            line[8 + 16 * b : 24 + 16 * b] = src_ref[b, col]
        line[264:280] = src_ref[0, col]
        near = 1.0 - frac
        for m in range(32):
            start = ((8 * m - cells) & 255) + 8
            value = near * line[pl.ds(start, 8)] + frac * line[pl.ds(start - 1, 8)]
            out_ref[m // 2, pl.ds(pl.multiple_of(row + 8 * (m % 2), 8), 8)] = value

    @pl.loop(0, 8)
    def _(col):
        one(col, 0, 16 * col)

    @pl.loop(0, 2)
    def _(e):
        one(e + 6 * half, side, 160 + 16 * e)

    sub = lax.broadcasted_iota(jnp.int32, (8, 128), 0)
    top = sub < 4
    own = (sub < 2) | (sub >= 6)

    @pl.loop(0, 4)
    def _(c):
        for d in range(16):
            lo, hi = (d + 15) % 16, (d + 1) % 16
            a = pl.multiple_of(16 * c, 16)
            b = pl.multiple_of(16 * c + 64, 16)
            one_halo = jnp.where(top, out_ref[hi, pl.ds(a, 8)], out_ref[lo, pl.ds(a + 8, 8)])
            two_halo = jnp.where(top, out_ref[hi, pl.ds(b, 8)], out_ref[lo, pl.ds(b + 8, 8)])
            out_ref[d, pl.ds(pl.multiple_of(128 + 8 * c, 8), 8)] = jnp.where(
                own, one_halo, pltpu.roll(two_halo, 4, 0)
            )


def limited(a, b):
    return jnp.maximum(jnp.minimum(a, b), 0.0) + jnp.minimum(jnp.maximum(a, b), 0.0)


def face_difference(qs, vs):
    m2, m1, q, p1, p2 = qs
    vm, v, vp = vs
    d0, d1, d2, d3 = m1 - m2, q - m1, p1 - q, p2 - p1
    s0, s1, s2 = 0.5 * limited(d0, d1), 0.5 * limited(d1, d2), 0.5 * limited(d2, d3)
    a_lo, a_hi = 0.5 * (vm + v), 0.5 * (v + vp)
    lo = a_lo * jnp.where(a_lo > 0, m1 + s0, q - s1)
    hi = a_hi * jnp.where(a_hi > 0, q + s1, p1 - s2)
    return hi - lo


def update_kernel(t_ref, lo_ref, hi_ref, p_ref, out_ref, q_ref, vx_ref, vy_ref):
    gy = lax.axis_index("gy")
    lane = lax.broadcasted_iota(jnp.int32, (16, 128), 1)
    low_half = lane < 64
    zc = GRAVITY * (((lane + gy * 128).astype(jnp.float32) + 0.5) / NZ - 0.5)
    for f in range(8):
        for e in range(2):
            q_ref[f, e, 8:24] = lo_ref[f, 16 * e : 16 * e + 16]
            q_ref[f, 18 + e, 8:24] = hi_ref[f, 16 * e : 16 * e + 16]
        for h in range(2):
            for c in range(8):
                q_ref[f, 2 + 8 * h + c, 8:24] = t_ref[2 * f + h, 16 * c : 16 * c + 16]
            for c in range(4):
                tile = t_ref[2 * f + h, 128 + 8 * c : 136 + 8 * c]
                q_ref[f, 2 + 8 * h + c, 0:8] = tile
                q_ref[f, 2 + 8 * h + c, 24:32] = tile
                tile = pltpu.roll(tile, 4, 0)
                q_ref[f, 6 + 8 * h + c, 0:8] = tile
                q_ref[f, 6 + 8 * h + c, 24:32] = tile

    @pl.loop(1, 19)
    def _(x):
        vx_ref[x] = q_ref[1, x, 8:24] / q_ref[0, x, 8:24]

    @pl.loop(0, 16)
    def _(x):
        vy_ref[...] = q_ref[2, x + 2] / q_ref[0, x + 2]
        vys = [vy_ref[7 + k : 23 + k] for k in range(3)]
        vxs = [vx_ref[x + 1 + k] for k in range(3)]
        half, col = x // 8, lax.rem(x, 8)
        row = pl.multiple_of(16 * col, 16)

        def edges(f):
            q = q_ref[f, x + 2, 8:24]
            other = p_ref[2 * f + half, pl.ds(row, 16)]
            first = jnp.broadcast_to(q[:, 0:1], (16, 128))
            final = jnp.broadcast_to(q[:, 127:128], (16, 128))
            edge = jnp.where(gy == 0, first, final)
            return q, jnp.where(low_half == (gy == 0), other, edge)

        def shifted(q, p):
            return [
                pltpu.roll(jnp.where(lane >= 126, p, q), 2, 1),
                pltpu.roll(jnp.where(lane >= 127, p, q), 1, 1),
                q,
                pltpu.roll(jnp.where(lane < 1, p, q), 127, 1),
                pltpu.roll(jnp.where(lane < 2, p, q), 126, 1),
            ]

        q0, p0 = edges(0)
        q3, p3 = edges(3)
        vzs = shifted(q3 / q0, p3 / p0)[1:4]
        for f in range(8):
            q, p = edges(f)
            total = face_difference(shifted(q, p), vzs)
            total += face_difference([q_ref[f, x, 8:24], q_ref[f, x + 1, 8:24], q,
                                      q_ref[f, x + 3, 8:24], q_ref[f, x + 4, 8:24]], vxs)
            total += face_difference([q_ref[f, x + 2, 6 + k : 22 + k] for k in range(5)], vys)
            new = q - DT * total
            if f == 3:
                new -= DT * zc * q0
            out_ref[f, x] = new


def local(fields, col_cells, col_num, shear_sub):
    pieces = fields.reshape(NB, 8, 16, 128)
    lines = lax.all_to_all(pieces, "gx", 0, 0, tiled=True)
    send = pl.pallas_call(
        shift_kernel,
        out_shape=jax.ShapeDtypeStruct((NB, 192, 128), jnp.float32),
        in_specs=[SMEM, SMEM, SMEM, VMEM],
        out_specs=VMEM,
        scratch_shapes=[pltpu.VMEM((280, 128), jnp.float32)],
        compiler_params=pltpu.CompilerParams(vmem_limit_bytes=16 * 2**20),
        name="shift",
    )(col_cells, col_num, shear_sub, lines)
    t = lax.all_to_all(send, "gx", 0, 0, tiled=True)
    count = lax.axis_size("gz")
    up = [(i, (i + 1) % count) for i in range(count)]
    down = [(b, a) for a, b in up]
    by_half = t.reshape(8, 2, 192, 128)
    lo = lax.ppermute(by_half[:, 1, 160:], "gz", up)
    hi = lax.ppermute(by_half[:, 0, 160:], "gz", down)
    partner = lax.ppermute(t[:, :128], "gy", [(0, 1), (1, 0)])
    return pl.pallas_call(
        update_kernel,
        out_shape=jax.ShapeDtypeStruct((8, 16, 16, 128), jnp.float32),
        in_specs=[VMEM] * 4,
        out_specs=VMEM,
        scratch_shapes=[
            pltpu.VMEM((8, 20, 32, 128), jnp.float32),
            pltpu.VMEM((20, 16, 128), jnp.float32),
            pltpu.VMEM((32, 128), jnp.float32),
        ],
        compiler_params=pltpu.CompilerParams(vmem_limit_bytes=32 * 2**20),
        name="update",
    )(t, lo, hi, partner)


def solution(mesh):
    return jax.shard_map(
        local,
        mesh=mesh,
        in_specs=(P(None, "gz", "gx", "gy"), P(), P(), P()),
        out_specs=P(None, "gz", "gx", "gy"),
        check_vma=False,
    )
```

time: 244 us -> 71.6 us (0.29)
  waiting for transfers between devices: 149 us -> 21.3 us
  local copies, waits for them, and re-layouts: 47.3 us -> 0.11 us
  blocking collectives: 0 us -> 25.6 us
  other arithmetic: 21.8 us -> 0 us
  between operations: 14.3 us -> 0.68 us
  Pallas kernels: 0 us -> 8.05 us
  starting transfers between devices: 11.2 us -> 15.6 us
    all_gather x1 -> x0, waiting for transfers between devices: 136 us -> none  [local(): piece = lax.all_gather(extended, 'gx', axis=2, tiled=True)]
    all_to_all x0 -> x1, blocking collectives: none -> 25.6 us  [local(): t = lax.all_to_all(send, 'gx', 0, 0, tiled=True)]
    gather x6 -> x0, local copies, waits for them, and re-layouts: 25.1 us -> none  [the longest x3 12.5 us: local(): jnp.take_along_axis(piece, jnp.clip(first, 0, count - 1)[None, :, :, None...]
    all_to_all x0 -> x1, waiting for transfers between devices: none -> 15.3 us  [local(): lines = lax.all_to_all(pieces, 'gx', 0, 0, tiled=True)]
    slice x9 -> x1, local copies, waits for them, and re-layouts: 9.9 us -> 0.09 us  [local(): partner = lax.ppermute(t[:, :128], 'gy', [(0, 1), (1, 0)])]
    pallas_call x0 -> x2, Pallas kernels: none -> 8.05 us  [the longest x1 6.74 us: local(): pl.pallas_call(update_kernel, out_shape=jax.ShapeDtypeStruct((8, 16, 16,...]
    select_n x4 -> x0, other arithmetic: 7.76 us -> none  [the longest x1 4.97 us: local(): jnp.where(bottom[None, None, None, :], padded[:, :, :, 2:3], padded)]
    all_to_all x0 -> x1, starting transfers between devices: none -> 7.72 us  [local(): lines = lax.all_to_all(pieces, 'gx', 0, 0, tiled=True)]
  transfers between devices with their start and end apart: 7 -> 4, of which waited for: 5 -> 3; matrix products, arithmetic and copies ran while one was open for 3% -> 0% of each run, Pallas kernels for 0% -> 0%
where the time goes in v1:
time: 71.6 us; the launch traced here: 71.4 us
  blocking collectives  25.6 us (36%)
  waiting for transfers between devices  21.3 us (30%)
  starting transfers between devices  15.6 us (22%)
  Pallas kernels  8.05 us (11%)
    all_to_all x1, blocking collectives, local(): t = lax.all_to_all(send, 'gx', 0, 0, tiled=True)  25.6 us
    all_to_all x1, waiting for transfers between devices, local(): lines = lax.all_to_all(pieces, 'gx', 0, 0, tiled=True)  15.3 us
    all_to_all x1, starting transfers between devices, local(): lines = lax.all_to_all(pieces, 'gx', 0, 0, tiled=True)  7.72 us
    pallas_call x1, Pallas kernels, local(): pl.pallas_call(update_kernel, out_shape=jax.ShapeDtypeStruct((8, 16, 16,...  6.74 us
    ppermute x1, starting transfers between devices, local(): hi = lax.ppermute(by_half[:, 0, 160:], 'gz', down)  5.65 us
    ppermute x1, waiting for transfers between devices, local(): lo = lax.ppermute(by_half[:, 1, 160:], 'gz', up)  3.09 us
    ppermute x1, waiting for transfers between devices, local(): hi = lax.ppermute(by_half[:, 0, 160:], 'gz', down)  2.91 us
    ppermute x1, starting transfers between devices, local(): partner = lax.ppermute(t[:, :128], 'gy', [(0, 1), (1, 0)])  2.21 us
  transfers between devices with their start and end apart: 4, of which 3 were waited for; matrix products, arithmetic and copies ran while one was open for 0% of the time, Pallas kernels for 0%

profile of v1, /device:TPU:1, one launch (start us, length us, event | category | flops | bytes accessed | tf_op | source)
XLA Modules:
  0.0 71.4 jit_solution(10229227082406699670)
XLA Ops:
  0.0 0.0 copy-start.1
  0.0 0.0 copy-start
  0.0 7.7 %all-to-all-start = ((f32[16,8,16,128]{3,2,1,0:T(8,128)}), f32[16,8,16,128]{3,2,1,0:T(8,128)S(1)}, u32[]{:S(2)}, u32[]{:S(2)}) async-start(f32[16,8,16,128]{3,2,1,0:T(8,128)} %bitcast.11), calls=%async_computation | async-start | bytes 2097152 | tf_op jit(solution)/shard_map/all_to_all | solution.py:146
  8.4 15.3 %all-to-all-done.src_ref = f32[16,8,16,128]{3,2,1,0:T(8,128)S(1)} async-done(((f32[16,8,16,128]{3,2,1,0:T(8,128)}), f32[16,8,16,128]{3,2,1,0:T(8,128)S(1)}, u32[]{:S(2)}, u32[]{:S(2)}) %all-to-all-start) | async-done | bytes 1048608 | tf_op jit(solution)/shard_map/all_to_all | solution.py:146
  23.7 0.0 copy-done.1
  23.7 0.0 copy-done
  23.7 1.3 %shift.1 = f32[16,192,128]{2,1,0:T(8,128)S(1)} custom-call(s32[128]{0:T(128)S(1)} %copy-done, s32[128]{0:T(128)S(1)} %copy-done.1, s32[1]{0:T(128)S(6)} %copy.9.shear_ref, f32[16,8,16,128]{3,2,1,0:T(8,128)S(1)} %all-to-all-done.src_ref), custom_call_target="tpu_custom_call" | custom-call | tf_op jit(solution)/shard_map/shift/pallas_call | solution.py:147
  25.0 25.6 %all_to_all.10.t_ref = f32[16,192,128]{2,1,0:T(8,128)S(1)} all-to-all(f32[16,192,128]{2,1,0:T(8,128)S(1)} %shift.1), channel_id=1, replica_groups=mesh['gx'=16,'gy'=2,'gz'=8] {'gx'}, dimensions={0} | all-to-all | bytes 3145728 | tf_op jit(solution)/shard_map/all_to_all | solution.py:156
  50.6 0.1 slice.14
  50.7 2.2 %collective-permute-start.2 = (f32[16,128,128]{2,1,0:T(8,128)S(1)}, f32[16,128,128]{2,1,0:T(8,128)S(1)}, u32[]{:S(2)}, u32[]{:S(2)}) collective-permute-start(f32[16,128,128]{2,1,0:T(8,128)S(1)} %slice.14), channel_id=1, source_target_pairs={{0,8},{8,0},{1,9},{9,1},{2,10},{10,2},{3,11},{11,3},{4,12},{12,4},... | collective-permute-start | bytes 3145736 | tf_op jit(solution)/shard_map/ppermute | solution.py:163
  53.0 5.7 %collective-permute-start.1 = (f32[8,32,128]{2,1,0:T(8,128)S(1)}, f32[8,32,128]{2,1,0:T(8,128)S(1)}, u32[]{:S(2)}, u32[]{:S(2)}) collective-permute-start(f32[8,32,128]{2,1,0:T(8,128)S(1)} %get-tuple-element.5), channel_id=1, source_target_pairs={{1,0},{2,1},{3,2},{4,3},{5,4},{6,5},{7,6},{0,7},{9,8},{10,9},{11,1... | collective-permute-start | bytes 393224 | tf_op jit(solution)/shard_map/ppermute | solution.py:162
  58.6 0.0 collective-permute-start
  58.6 2.9 %collective-permute-done.1.hi_ref = f32[8,32,128]{2,1,0:T(8,128)S(1)} collective-permute-done((f32[8,32,128]{2,1,0:T(8,128)S(1)}, f32[8,32,128]{2,1,0:T(8,128)S(1)}, u32[]{:S(2)}, u32[]{:S(2)}) %collective-permute-start.1) | collective-permute-done | bytes 131104 | tf_op jit(solution)/shard_map/ppermute | solution.py:162
  61.5 3.1 %collective-permute-done.lo_ref = f32[8,32,128]{2,1,0:T(8,128)S(1)} collective-permute-done((f32[8,32,128]{2,1,0:T(8,128)S(1)}, f32[8,32,128]{2,1,0:T(8,128)S(1)}, u32[]{:S(2)}, u32[]{:S(2)}) %collective-permute-start) | collective-permute-done | bytes 131104 | tf_op jit(solution)/shard_map/ppermute | solution.py:161
  64.6 0.0 collective-permute-done.2.p_ref
  64.6 6.7 %update.1 = f32[8,16,16,128]{3,2,1,0:T(8,128)} custom-call(f32[16,192,128]{2,1,0:T(8,128)S(1)} %all_to_all.10.t_ref, f32[8,32,128]{2,1,0:T(8,128)S(1)} %collective-permute-done.lo_ref, f32[8,32,128]{2,1,0:T(8,128)S(1)} %collective-permute-done.1.hi_ref, f32[16,128,128]{2,1,0:T(8,128)S(1)} %collective-permute-done.2.p_ref), custom_call_target="tpu_custom_call" | custom-call | tf_op jit(solution)/shard_map/update/pallas_call | solution.py:164
  (1 shorter events, 0.0 us)
Async XLA Ops:
  0.0 23.7 %copy-start.1 = (s32[128]{0:T(128)S(1)}, s32[128]{0:T(128)}, u32[]{:S(2)}) copy-start(s32[128]{0:T(128)} %num_ref.1) | copy-start | bytes 1540
  0.0 23.7 %copy-start = (s32[128]{0:T(128)S(1)}, s32[128]{0:T(128)}, u32[]{:S(2)}) copy-start(s32[128]{0:T(128)} %cells_ref.1) | copy-start | bytes 1540
  0.0 23.7 %all-to-all-start = ((f32[16,8,16,128]{3,2,1,0:T(8,128)}), f32[16,8,16,128]{3,2,1,0:T(8,128)S(1)}, u32[]{:S(2)}, u32[]{:S(2)}) async-start(f32[16,8,16,128]{3,2,1,0:T(8,128)} %bitcast.11), calls=%async_computation | async-start | bytes 2097152 | tf_op jit(solution)/shard_map/all_to_all | solution.py:146
  50.7 13.9 %collective-permute-start.2 = (f32[16,128,128]{2,1,0:T(8,128)S(1)}, f32[16,128,128]{2,1,0:T(8,128)S(1)}, u32[]{:S(2)}, u32[]{:S(2)}) collective-permute-start(f32[16,128,128]{2,1,0:T(8,128)S(1)} %slice.14), channel_id=1, source_target_pairs={{0,8},{8,0},{1,9},{9,1},{2,10},{10,2},{3,11},{11,3},{4,12},{12,4},... | collective-permute-start | bytes 3145736 | tf_op jit(solution)/shard_map/ppermute | solution.py:163
  53.0 8.6 %collective-permute-start.1 = (f32[8,32,128]{2,1,0:T(8,128)S(1)}, f32[8,32,128]{2,1,0:T(8,128)S(1)}, u32[]{:S(2)}, u32[]{:S(2)}) collective-permute-start(f32[8,32,128]{2,1,0:T(8,128)S(1)} %get-tuple-element.5), channel_id=1, source_target_pairs={{1,0},{2,1},{3,2},{4,3},{5,4},{6,5},{7,6},{0,7},{9,8},{10,9},{11,1... | collective-permute-start | bytes 393224 | tf_op jit(solution)/shard_map/ppermute | solution.py:162
  58.6 6.0 %collective-permute-start = (f32[8,32,128]{2,1,0:T(8,128)S(1)}, f32[8,32,128]{2,1,0:T(8,128)S(1)}, u32[]{:S(2)}, u32[]{:S(2)}) collective-permute-start(f32[8,32,128]{2,1,0:T(8,128)S(1)} %get-tuple-element.6), channel_id=1, source_target_pairs={{0,1},{1,2},{2,3},{3,4},{4,5},{5,6},{6,7},{7,0},{8,9},{9,10},{10,1... | collective-permute-start | bytes 393224 | tf_op jit(solution)/shard_map/ppermute | solution.py:161

commit v2 on v1

v2 whole, which is shorter than its diff:
```python
import jax
import jax.numpy as jnp
from jax import lax
from jax.experimental import pallas as pl
from jax.experimental.pallas import tpu as pltpu
from jax.sharding import PartitionSpec as P

DT = 0.2
GRAVITY = 4.0
NZ = 256
NB = 16
VMEM = pl.BlockSpec(memory_space=pltpu.VMEM)
SMEM = pl.BlockSpec(memory_space=pltpu.SMEM)


def shift_kernel(cells_ref, num_ref, shear_ref, src_ref, out_ref, line):
    gz = lax.axis_index("gz")
    last = lax.axis_size("gz") - 1
    half = lax.rem(lax.axis_index("gx"), 2)
    first_col = gz * 16 + half * 8
    shear = shear_ref[0]
    side = jnp.where(
        half == 1, jnp.where(gz == last, shear, 0), jnp.where(gz == 0, -shear, 0)
    )

    def one(col, extra, row):
        total = 64 * cells_ref[first_col + col] + num_ref[first_col + col] + extra
        cells = (total >> 6) & 255
        frac = (total & 63).astype(jnp.float32) * (1.0 / 64.0)
        line[0:8] = src_ref[15, col, 8:16]
        for b in range(16):
            line[8 + 16 * b : 24 + 16 * b] = src_ref[b, col]
        line[264:280] = src_ref[0, col]
        near = 1.0 - frac
        for m in range(32):
            start = ((8 * m - cells) & 255) + 8
            value = near * line[pl.ds(start, 8)] + frac * line[pl.ds(start - 1, 8)]
            out_ref[m // 2, pl.ds(pl.multiple_of(row + 8 * (m % 2), 8), 8)] = value

    @pl.loop(0, 8)
    def _(col):
        one(col, 0, 16 * col)

    @pl.loop(0, 2)
    def _(e):
        one(e + 6 * half, side, 160 + 16 * e)

    sub = lax.broadcasted_iota(jnp.int32, (8, 128), 0)
    top = sub < 4
    own = (sub < 2) | (sub >= 6)

    @pl.loop(0, 4)
    def _(c):
        for d in range(16):
            lo, hi = (d + 15) % 16, (d + 1) % 16
            a = pl.multiple_of(16 * c, 16)
            b = pl.multiple_of(16 * c + 64, 16)
            one_halo = jnp.where(top, out_ref[hi, pl.ds(a, 8)], out_ref[lo, pl.ds(a + 8, 8)])
            two_halo = jnp.where(top, out_ref[hi, pl.ds(b, 8)], out_ref[lo, pl.ds(b + 8, 8)])
            out_ref[d, pl.ds(pl.multiple_of(128 + 8 * c, 8), 8)] = jnp.where(
                own, one_halo, pltpu.roll(two_halo, 4, 0)
            )


def limited(a, b):
    return jnp.maximum(jnp.minimum(a, b), 0.0) + jnp.minimum(jnp.maximum(a, b), 0.0)


def upwind(a, left, right):
    return a * jnp.where(a > 0, left, right)


def cells_of(t_ref, f, x):
    return t_ref[2 * f + x // 8, 16 * (x % 8) : 16 * (x % 8) + 16]


def ring_of(t_ref, f, x):
    c = x % 4
    tile = t_ref[2 * f + x // 8, 128 + 8 * c : 136 + 8 * c]
    if x % 8 >= 4:
        tile = pltpu.roll(tile, 4, 0)
    return jnp.concatenate([tile, cells_of(t_ref, f, x)], axis=0)


def inner_kernel(t_ref, out_ref, ax_ref, ay_ref):
    before = None
    for x in range(16):
        density = ring_of(t_ref, 0, x)
        inverse = 1.0 / density
        vy = ring_of(t_ref, 2, x) * inverse
        ay_ref[x] = 0.5 * (vy + pltpu.roll(vy, 1, 0))
        vx = cells_of(t_ref, 1, x) * inverse[8:]
        if x:
            ax_ref[x] = 0.5 * (vx + before)
        before = vx

    @pl.loop(0, 8)
    def _(f):
        qs, ds, fluxes, totals = {}, {}, {}, {}
        last = None
        for x in range(16):
            ring = ring_of(t_ref, f, x)
            d = ring - pltpu.roll(ring, 1, 0)
            h = 0.5 * limited(d, pltpu.roll(d, 23, 0))
            flux = upwind(ay_ref[x], pltpu.roll(ring + h, 1, 0), ring - h)
            totals[x] = (pltpu.roll(flux, 23, 0) - flux)[8:]
            q = ring[8:]
            qs[x] = q
            if x >= 1:
                ds[x] = q - qs[x - 1]
            if x >= 2:
                h = 0.5 * limited(ds[x - 1], ds[x])
                if x >= 3:
                    fluxes[x - 1] = upwind(ax_ref[x - 1], last, qs[x - 1] - h)
                last = qs[x - 1] + h
            if x >= 4:
                totals[x - 2] += fluxes[x - 1] - fluxes[x - 2]
            if x >= 2:
                out_ref[f, x - 2] = qs[x - 2] - DT * totals[x - 2]
        for x in (14, 15):
            out_ref[f, x] = qs[x] - DT * totals[x]


def height_kernel(t_ref, p_ref, acc_ref, out_ref, edge_ref, lo_ref, hi_ref):
    gy = lax.axis_index("gy")
    lane = lax.broadcasted_iota(jnp.int32, (16, 128), 1)
    first, final = lane == 0, lane == 127

    def parts(q, p, low):
        if low:
            below = jnp.where(first, q, pltpu.roll(q, 1, 1))
            above = pltpu.roll(jnp.where(first, p, q), 127, 1)
        else:
            below = pltpu.roll(jnp.where(final, p, q), 1, 1)
            above = jnp.where(final, q, pltpu.roll(q, 127, 1))
        return below, above

    def run(low):
        for x in range(16):
            v = cells_of(t_ref, 3, x) / cells_of(t_ref, 0, x)
            vp = cells_of(p_ref, 3, x) / cells_of(p_ref, 0, x)
            below, above = parts(v, vp, low)
            lo_ref[x] = 0.5 * (below + v)
            hi_ref[x] = 0.5 * (v + above)

        @pl.loop(0, 8)
        def _(f):
            for x in range(16):
                q, p = cells_of(t_ref, f, x), cells_of(p_ref, f, x)
                below, above = parts(q, p, low)
                d0, d1 = q - below, above - q
                h = 0.5 * limited(d0, d1)
                left, right = q + h, q - h
                if low:
                    left_below = jnp.where(first, q, pltpu.roll(left, 1, 1))
                    far = pltpu.roll(p, 126, 1)
                    right_above = jnp.where(
                        final, above - 0.5 * limited(d1, far - above), pltpu.roll(right, 127, 1)
                    )
                else:
                    far = pltpu.roll(p, 2, 1)
                    left_below = jnp.where(
                        first, below + 0.5 * limited(below - far, d0), pltpu.roll(left, 1, 1)
                    )
                    right_above = jnp.where(final, q, pltpu.roll(right, 127, 1))
                flux = upwind(hi_ref[x], left, right_above) - upwind(lo_ref[x], left_below, right)
                new = acc_ref[f, x] - DT * flux
                out_ref[f, x] = new
                if x in EDGES:
                    edge_ref[f, EDGES.index(x)] = new

    pl.when(gy == 0)(lambda: run(True))
    pl.when(gy == 1)(lambda: run(False))
    zc = GRAVITY * (((lane + gy * 128).astype(jnp.float32) + 0.5) / NZ - 0.5)
    for x in range(16):
        new = out_ref[3, x] - DT * zc * cells_of(t_ref, 0, x)
        out_ref[3, x] = new
        if x in EDGES:
            edge_ref[3, EDGES.index(x)] = new


EDGES = (0, 1, 14, 15)


def edge_kernel(t_ref, lo_ref, hi_ref, edge_ref, _, out_ref):
    def run(columns, base):
        vs = []
        for k in range(1, 5):
            vs.append(columns(1, k) / columns(0, k))
        faces = [0.5 * (vs[k] + vs[k + 1]) for k in range(3)]

        @pl.loop(0, 8)
        def _(f):
            qs = [columns(f, k) for k in range(6)]
            hs = [0.5 * limited(qs[k] - qs[k - 1], qs[k + 1] - qs[k]) for k in range(1, 5)]
            fluxes = [
                upwind(faces[k], qs[k + 1] + hs[k], qs[k + 2] - hs[k + 1]) for k in range(3)
            ]
            for k in range(2):
                out_ref[f, k] = edge_ref[f, base + k] - DT * (fluxes[k + 1] - fluxes[k])

    @pl.when(pl.program_id(0) == 0)
    def _():
        run(lambda f, k: lo_ref[f, 16 * k : 16 * k + 16] if k < 2 else cells_of(t_ref, f, k - 2), 0)

    @pl.when(pl.program_id(0) == 1)
    def _():
        run(lambda f, k: hi_ref[f, 16 * k - 64 : 16 * k - 48] if k > 3 else cells_of(t_ref, f, k + 12), 2)


def local(fields, col_cells, col_num, shear_sub):
    pieces = fields.reshape(NB, 8, 16, 128)
    lines = lax.all_to_all(pieces, "gx", 0, 0, tiled=True)
    send = pl.pallas_call(
        shift_kernel,
        out_shape=jax.ShapeDtypeStruct((NB, 192, 128), jnp.float32),
        in_specs=[SMEM, SMEM, SMEM, VMEM],
        out_specs=VMEM,
        scratch_shapes=[pltpu.VMEM((280, 128), jnp.float32)],
        compiler_params=pltpu.CompilerParams(vmem_limit_bytes=16 * 2**20),
        name="shift",
    )(col_cells, col_num, shear_sub, lines)
    t = lax.all_to_all(send, "gx", 0, 0, tiled=True)
    count = lax.axis_size("gz")
    up = [(i, (i + 1) % count) for i in range(count)]
    down = [(b, a) for a, b in up]
    by_half = t.reshape(8, 2, 192, 128)
    lo = lax.ppermute(by_half[:, 1, 160:], "gz", up)
    hi = lax.ppermute(by_half[:, 0, 160:], "gz", down)
    partner = lax.ppermute(t[:, :128], "gy", [(0, 1), (1, 0)])
    block = jax.ShapeDtypeStruct((8, 16, 16, 128), jnp.float32)
    edges = jax.ShapeDtypeStruct((8, 4, 16, 128), jnp.float32)
    cost = pl.CostEstimate(flops=20_000_000, bytes_accessed=4_000_000, transcendentals=0)
    acc = pl.pallas_call(
        inner_kernel,
        out_shape=block,
        in_specs=[VMEM],
        out_specs=VMEM,
        scratch_shapes=[
            pltpu.VMEM((16, 16, 128), jnp.float32),
            pltpu.VMEM((16, 24, 128), jnp.float32),
        ],
        compiler_params=pltpu.CompilerParams(vmem_limit_bytes=16 * 2**20),
        cost_estimate=cost,
        name="inner",
    )(t)
    out, edge = pl.pallas_call(
        height_kernel,
        out_shape=[block, edges],
        in_specs=[VMEM] * 3,
        out_specs=[VMEM] * 2,
        scratch_shapes=[pltpu.VMEM((16, 16, 128), jnp.float32)] * 2,
        compiler_params=pltpu.CompilerParams(vmem_limit_bytes=16 * 2**20),
        cost_estimate=cost,
        name="height",
    )(t, partner, acc)
    return pl.pallas_call(
        edge_kernel,
        out_shape=block,
        grid=(2,),
        in_specs=[VMEM] * 4 + [pl.BlockSpec(memory_space=pl.ANY)],
        out_specs=pl.BlockSpec((8, 2, 16, 128), lambda i: (0, 7 * i, 0, 0)),
        input_output_aliases={4: 0},
        compiler_params=pltpu.CompilerParams(vmem_limit_bytes=16 * 2**20),
        name="edge",
    )(t, lo, hi, edge, out)


def solution(mesh):
    return jax.shard_map(
        local,
        mesh=mesh,
        in_specs=(P(None, "gz", "gx", "gy"), P(), P(), P()),
        out_specs=P(None, "gz", "gx", "gy"),
        check_vma=False,
    )
```

time: 71.6 us -> 65.3 us (0.912)
  waiting for transfers between devices: 21.3 us -> 15.3 us
    ppermute x1, waiting for transfers between devices: 3.09 us -> 0.01 us  [local(): lo = lax.ppermute(by_half[:, 1, 160:], 'gz', up)]
    ppermute x1, waiting for transfers between devices: 2.91 us -> 0.01 us  [local(): hi = lax.ppermute(by_half[:, 0, 160:], 'gz', down)]
    ppermute x1, starting transfers between devices: 0.01 us -> 1.71 us  [local(): lo = lax.ppermute(by_half[:, 1, 160:], 'gz', up)]
    ppermute x1, starting transfers between devices: 5.65 us -> 4.03 us  [local(): hi = lax.ppermute(by_half[:, 0, 160:], 'gz', down)]
    pallas_call x1 -> x3, Pallas kernels: 6.74 us -> 6.39 us  [the longest x1 3.73 us: local(): pl.pallas_call(height_kernel, out_shape=[block, edges], in_specs=[VMEM] *...]
  transfers between devices with their start and end apart: 4 -> 4, of which waited for: 3 -> 1; matrix products, arithmetic and copies ran while one was open for 0% -> 0% of each run, Pallas kernels for 0% -> 8%
where the time goes in v2:
time: 65.3 us; the launch traced here: 65.1 us
  blocking collectives  25.6 us (39%)
  starting transfers between devices  15.7 us (24%)
  waiting for transfers between devices  15.3 us (23%)
  Pallas kernels  7.69 us (12%)
  between operations  0.69 us (1%)
    all_to_all x1, blocking collectives, local(): t = lax.all_to_all(send, 'gx', 0, 0, tiled=True)  25.6 us
    all_to_all x1, waiting for transfers between devices, local(): lines = lax.all_to_all(pieces, 'gx', 0, 0, tiled=True)  15.3 us
    all_to_all x1, starting transfers between devices, local(): lines = lax.all_to_all(pieces, 'gx', 0, 0, tiled=True)  7.72 us
    ppermute x1, starting transfers between devices, local(): hi = lax.ppermute(by_half[:, 0, 160:], 'gz', down)  4.03 us
    pallas_call x1, Pallas kernels, local(): pl.pallas_call(height_kernel, out_shape=[block, edges], in_specs=[VMEM] *...  3.73 us
    ppermute x1, starting transfers between devices, local(): partner = lax.ppermute(t[:, :128], 'gy', [(0, 1), (1, 0)])  2.21 us
    ppermute x1, starting transfers between devices, local(): lo = lax.ppermute(by_half[:, 1, 160:], 'gz', up)  1.71 us
    pallas_call x1, Pallas kernels, local(): pl.pallas_call(inner_kernel, out_shape=block, in_specs=[VMEM], out_specs=...  1.63 us
  transfers between devices with their start and end apart: 4, of which 1 were waited for; matrix products, arithmetic and copies ran while one was open for 0% of the time, Pallas kernels for 8%

profile of v2, /device:TPU:1, one launch (start us, length us, event | category | flops | bytes accessed | tf_op | source)
XLA Modules:
  0.0 65.1 jit_solution(4683394663576332873)
XLA Ops:
  0.0 0.0 copy-start
  0.0 0.0 copy-start.1
  0.0 7.7 %all-to-all-start = ((f32[16,8,16,128]{3,2,1,0:T(8,128)}), f32[16,8,16,128]{3,2,1,0:T(8,128)S(1)}, u32[]{:S(2)}, u32[]{:S(2)}) async-start(f32[16,8,16,128]{3,2,1,0:T(8,128)} %bitcast.11), calls=%async_computation | async-start | bytes 2097152 | tf_op jit(solution)/shard_map/all_to_all | solution.py:213
  8.4 15.3 %all-to-all-done.src_ref = f32[16,8,16,128]{3,2,1,0:T(8,128)S(1)} async-done(((f32[16,8,16,128]{3,2,1,0:T(8,128)}), f32[16,8,16,128]{3,2,1,0:T(8,128)S(1)}, u32[]{:S(2)}, u32[]{:S(2)}) %all-to-all-start) | async-done | bytes 1048608 | tf_op jit(solution)/shard_map/all_to_all | solution.py:213
  23.7 0.0 copy-done
  23.7 0.0 copy-done.1
  23.7 1.3 %shift.1 = f32[16,192,128]{2,1,0:T(8,128)S(1)} custom-call(s32[128]{0:T(128)S(1)} %copy-done, s32[128]{0:T(128)S(1)} %copy-done.1, s32[1]{0:T(128)S(6)} %copy.11.shear_ref, f32[16,8,16,128]{3,2,1,0:T(8,128)S(1)} %all-to-all-done.src_ref), custom_call_target="tpu_custom_call" | custom-call | tf_op jit(solution)/shard_map/shift/pallas_call | solution.py:214
  25.0 25.6 %all_to_all.10.t_ref = f32[16,192,128]{2,1,0:T(8,128)S(1)} all-to-all(f32[16,192,128]{2,1,0:T(8,128)S(1)} %shift.1), channel_id=1, replica_groups=mesh['gx'=16,'gy'=2,'gz'=8] {'gx'}, dimensions={0} | all-to-all | bytes 3145728 | tf_op jit(solution)/shard_map/all_to_all | solution.py:223
  50.6 0.1 slice.14
  50.7 2.2 %collective-permute-start.2 = (f32[16,128,128]{2,1,0:T(8,128)S(1)}, f32[16,128,128]{2,1,0:T(8,128)S(1)}, u32[]{:S(2)}, u32[]{:S(2)}) collective-permute-start(f32[16,128,128]{2,1,0:T(8,128)S(1)} %slice.14), channel_id=1, source_target_pairs={{0,8},{8,0},{1,9},{9,1},{2,10},{10,2},{3,11},{11,3},{4,12},{12,4},... | collective-permute-start | bytes 3145736 | tf_op jit(solution)/shard_map/ppermute | solution.py:230
  53.0 1.7 %collective-permute-start = (f32[8,32,128]{2,1,0:T(8,128)S(1)}, f32[8,32,128]{2,1,0:T(8,128)S(1)}, u32[]{:S(2)}, u32[]{:S(2)}) collective-permute-start(f32[8,32,128]{2,1,0:T(8,128)S(1)} %get-tuple-element.10), channel_id=1, source_target_pairs={{0,1},{1,2},{2,3},{3,4},{4,5},{5,6},{6,7},{7,0},{8,9},{9,10},{10,1... | collective-permute-start | bytes 393224 | tf_op jit(solution)/shard_map/ppermute | solution.py:228
  54.7 4.0 %collective-permute-start.1 = (f32[8,32,128]{2,1,0:T(8,128)S(1)}, f32[8,32,128]{2,1,0:T(8,128)S(1)}, u32[]{:S(2)}, u32[]{:S(2)}) collective-permute-start(f32[8,32,128]{2,1,0:T(8,128)S(1)} %get-tuple-element.9), channel_id=1, source_target_pairs={{1,0},{2,1},{3,2},{4,3},{5,4},{6,5},{7,6},{0,7},{9,8},{10,9},{11,1... | collective-permute-start | bytes 393224 | tf_op jit(solution)/shard_map/ppermute | solution.py:229
  58.7 1.6 %inner.1.acc_ref = f32[8,16,16,128]{3,2,1,0:T(8,128)S(1)} custom-call(f32[16,192,128]{2,1,0:T(8,128)S(1)} %all_to_all.10.t_ref), custom_call_target="tpu_custom_call" | custom-call | flops 20000000 | bytes 4000000 | tf_op jit(solution)/shard_map/inner/pallas_call | solution.py:234
  60.3 0.0 collective-permute-done.2.p_ref
  60.3 3.7 %height.1 = (f32[8,16,16,128]{3,2,1,0:T(8,128)}, f32[8,4,16,128]{3,2,1,0:T(8,128)S(1)}) custom-call(f32[16,192,128]{2,1,0:T(8,128)S(1)} %all_to_all.10.t_ref, f32[16,128,128]{2,1,0:T(8,128)S(1)} %collective-permute-done.2.p_ref, f32[8,16,16,128]{3,2,1,0:T(8,128)S(1)} %inner.1.acc_ref), custom_call_target="tpu_custom_call" | custom-call | flops 20000000 | bytes 4000000 | tf_op jit(solution)/shard_map/height/pallas_call | solution.py:247
  64.1 0.0 collective-permute-done.lo_ref
  64.1 0.0 collective-permute-done.1.hi_ref
  64.1 1.0 %edge.1 = f32[8,16,16,128]{3,2,1,0:T(8,128)} custom-call(f32[16,192,128]{2,1,0:T(8,128)S(1)} %all_to_all.10.t_ref, f32[8,32,128]{2,1,0:T(8,128)S(1)} %collective-permute-done.lo_ref, f32[8,32,128]{2,1,0:T(8,128)S(1)} %collective-permute-done.1.hi_ref, f32[8,4,16,128]{3,2,1,0:T(8,128)S(1)} %get-tuple-element.7.edge_ref, ...), custom_call_target="tpu_custom_call", output_to_operand_aliasing={{}: (4, {})} | custom-call | tf_op jit(solution)/shard_map/edge/pallas_call | solution.py:257
  (1 shorter events, 0.0 us)
Async XLA Ops:
  0.0 23.7 %copy-start = (s32[128]{0:T(128)S(1)}, s32[128]{0:T(128)}, u32[]{:S(2)}) copy-start(s32[128]{0:T(128)} %cells_ref.1) | copy-start | bytes 1540
  0.0 23.7 %copy-start.1 = (s32[128]{0:T(128)S(1)}, s32[128]{0:T(128)}, u32[]{:S(2)}) copy-start(s32[128]{0:T(128)} %num_ref.1) | copy-start | bytes 1540
  0.0 23.7 %all-to-all-start = ((f32[16,8,16,128]{3,2,1,0:T(8,128)}), f32[16,8,16,128]{3,2,1,0:T(8,128)S(1)}, u32[]{:S(2)}, u32[]{:S(2)}) async-start(f32[16,8,16,128]{3,2,1,0:T(8,128)} %bitcast.11), calls=%async_computation | async-start | bytes 2097152 | tf_op jit(solution)/shard_map/all_to_all | solution.py:213
  50.7 9.6 %collective-permute-start.2 = (f32[16,128,128]{2,1,0:T(8,128)S(1)}, f32[16,128,128]{2,1,0:T(8,128)S(1)}, u32[]{:S(2)}, u32[]{:S(2)}) collective-permute-start(f32[16,128,128]{2,1,0:T(8,128)S(1)} %slice.14), channel_id=1, source_target_pairs={{0,8},{8,0},{1,9},{9,1},{2,10},{10,2},{3,11},{11,3},{4,12},{12,4},... | collective-permute-start | bytes 3145736 | tf_op jit(solution)/shard_map/ppermute | solution.py:230
  53.0 11.1 %collective-permute-start = (f32[8,32,128]{2,1,0:T(8,128)S(1)}, f32[8,32,128]{2,1,0:T(8,128)S(1)}, u32[]{:S(2)}, u32[]{:S(2)}) collective-permute-start(f32[8,32,128]{2,1,0:T(8,128)S(1)} %get-tuple-element.10), channel_id=1, source_target_pairs={{0,1},{1,2},{2,3},{3,4},{4,5},{5,6},{6,7},{7,0},{8,9},{9,10},{10,1... | collective-permute-start | bytes 393224 | tf_op jit(solution)/shard_map/ppermute | solution.py:228
  54.7 9.4 %collective-permute-start.1 = (f32[8,32,128]{2,1,0:T(8,128)S(1)}, f32[8,32,128]{2,1,0:T(8,128)S(1)}, u32[]{:S(2)}, u32[]{:S(2)}) collective-permute-start(f32[8,32,128]{2,1,0:T(8,128)S(1)} %get-tuple-element.9), channel_id=1, source_target_pairs={{1,0},{2,1},{3,2},{4,3},{5,4},{6,5},{7,6},{0,7},{9,8},{10,9},{11,1... | collective-permute-start | bytes 393224 | tf_op jit(solution)/shard_map/ppermute | solution.py:229

commit v3 on v2

v3 whole, which is shorter than its diff:
```python
import jax
import jax.numpy as jnp
from jax import lax
from jax.experimental import pallas as pl
from jax.experimental.pallas import tpu as pltpu
from jax.sharding import PartitionSpec as P

DT = 0.2
GRAVITY = 4.0
NZ = 256
NB = 16
VMEM = pl.BlockSpec(memory_space=pltpu.VMEM)
SMEM = pl.BlockSpec(memory_space=pltpu.SMEM)


def shift_kernel(cells_ref, num_ref, shear_ref, src_ref, out_ref, line):
    gz = lax.axis_index("gz")
    last = lax.axis_size("gz") - 1
    half = lax.rem(lax.axis_index("gx"), 2)
    first_col = gz * 16 + half * 8
    shear = shear_ref[0]
    side = jnp.where(
        half == 1, jnp.where(gz == last, shear, 0), jnp.where(gz == 0, -shear, 0)
    )

    def one(col, extra, row):
        total = 64 * cells_ref[first_col + col] + num_ref[first_col + col] + extra
        cells = (total >> 6) & 255
        frac = (total & 63).astype(jnp.float32) * (1.0 / 64.0)
        line[0:8] = src_ref[15, col, 8:16]
        for b in range(16):
            line[8 + 16 * b : 24 + 16 * b] = src_ref[b, col]
        line[264:280] = src_ref[0, col]
        near = 1.0 - frac
        for m in range(32):
            start = ((8 * m - cells) & 255) + 8
            value = near * line[pl.ds(start, 8)] + frac * line[pl.ds(start - 1, 8)]
            out_ref[m // 2, pl.ds(pl.multiple_of(row + 8 * (m % 2), 8), 8)] = value

    @pl.loop(0, 8)
    def _(col):
        one(col, 0, 16 * col)

    @pl.loop(0, 2)
    def _(e):
        one(e + 6 * half, side, 160 + 16 * e)

    sub = lax.broadcasted_iota(jnp.int32, (8, 128), 0)
    top = sub < 4
    own = (sub < 2) | (sub >= 6)

    @pl.loop(0, 4)
    def _(c):
        for d in range(16):
            lo, hi = (d + 15) % 16, (d + 1) % 16
            a = pl.multiple_of(16 * c, 16)
            b = pl.multiple_of(16 * c + 64, 16)
            one_halo = jnp.where(top, out_ref[hi, pl.ds(a, 8)], out_ref[lo, pl.ds(a + 8, 8)])
            two_halo = jnp.where(top, out_ref[hi, pl.ds(b, 8)], out_ref[lo, pl.ds(b + 8, 8)])
            out_ref[d, pl.ds(pl.multiple_of(128 + 8 * c, 8), 8)] = jnp.where(
                own, one_halo, pltpu.roll(two_halo, 4, 0)
            )


def limited(a, b):
    return jnp.maximum(jnp.minimum(a, b), 0.0) + jnp.minimum(jnp.maximum(a, b), 0.0)


def upwind(a, left, right):
    return a * jnp.where(a > 0, left, right)


def cells_of(t_ref, f, x):
    return t_ref[2 * f + x // 8, 16 * (x % 8) : 16 * (x % 8) + 16]


def ring_of(t_ref, f, x):
    c = x % 4
    tile = t_ref[2 * f + x // 8, 128 + 8 * c : 136 + 8 * c]
    if x % 8 >= 4:
        tile = pltpu.roll(tile, 4, 0)
    return jnp.concatenate([tile, cells_of(t_ref, f, x)], axis=0)


EDGES = (0, 1, 14, 15)


def inner_kernel(t_ref, p_ref, out_ref, edge_ref, new_ref, ax_ref, ay_ref, lo_ref, hi_ref, sems):
    gy = lax.axis_index("gy")
    lane = lax.broadcasted_iota(jnp.int32, (16, 128), 1)
    first, final = lane == 0, lane == 127
    zc = GRAVITY * (((lane + gy * 128).astype(jnp.float32) + 0.5) / NZ - 0.5)

    def parts(q, p, low):
        if low:
            below = jnp.where(first, q, pltpu.roll(q, 1, 1))
            above = pltpu.roll(jnp.where(first, p, q), 127, 1)
        else:
            below = pltpu.roll(jnp.where(final, p, q), 1, 1)
            above = jnp.where(final, q, pltpu.roll(q, 127, 1))
        return below, above

    def z_flux(f, x, q, low):
        p = cells_of(p_ref, f, x)
        below, above = parts(q, p, low)
        d0, d1 = q - below, above - q
        h = 0.5 * limited(d0, d1)
        left, right = q + h, q - h
        if low:
            left_below = jnp.where(first, q, pltpu.roll(left, 1, 1))
            far = pltpu.roll(p, 126, 1)
            right_above = jnp.where(
                final, above - 0.5 * limited(d1, far - above), pltpu.roll(right, 127, 1)
            )
        else:
            far = pltpu.roll(p, 2, 1)
            left_below = jnp.where(
                first, below + 0.5 * limited(below - far, d0), pltpu.roll(left, 1, 1)
            )
            right_above = jnp.where(final, q, pltpu.roll(right, 127, 1))
        return upwind(hi_ref[x], left, right_above) - upwind(lo_ref[x], left_below, right)

    def run(low):
        before = None
        for x in range(16):
            density = ring_of(t_ref, 0, x)
            inverse = 1.0 / density
            vy = ring_of(t_ref, 2, x) * inverse
            ay_ref[x] = 0.5 * (vy + pltpu.roll(vy, 1, 0))
            vx = cells_of(t_ref, 1, x) * inverse[8:]
            if x:
                ax_ref[x] = 0.5 * (vx + before)
            before = vx
            vz = cells_of(t_ref, 3, x) * inverse[8:]
            vp = cells_of(p_ref, 3, x) / cells_of(p_ref, 0, x)
            below, above = parts(vz, vp, low)
            lo_ref[x] = 0.5 * (below + vz)
            hi_ref[x] = 0.5 * (vz + above)

        @pl.loop(0, 8)
        def _(f):
            qs, ds, fluxes, totals = {}, {}, {}, {}
            last = None
            weight = DT * (f == 3).astype(jnp.float32)

            def put(x):
                new = qs[x] - DT * totals[x]
                new_ref[f, x] = new
                if x in EDGES:
                    edge_ref[f, EDGES.index(x)] = new

            for x in range(16):
                ring = ring_of(t_ref, f, x)
                q = ring[8:]
                d = ring - pltpu.roll(ring, 1, 0)
                h = 0.5 * limited(d, pltpu.roll(d, 23, 0))
                flux = upwind(ay_ref[x], pltpu.roll(ring + h, 1, 0), ring - h)
                totals[x] = (pltpu.roll(flux, 23, 0) - flux)[8:] + z_flux(f, x, q, low)
                qs[x] = q
                if x >= 1:
                    ds[x] = q - qs[x - 1]
                if x >= 2:
                    h = 0.5 * limited(ds[x - 1], ds[x])
                    if x >= 3:
                        fluxes[x - 1] = upwind(ax_ref[x - 1], last, qs[x - 1] - h)
                    last = qs[x - 1] + h
                if x >= 4:
                    totals[x - 2] += fluxes[x - 1] - fluxes[x - 2]
                if x >= 2:
                    put(x - 2)
            put(14)
            put(15)

            @pl.when(f == 3)
            def _():
                for x in range(16):
                    new = new_ref[3, x] - DT * zc * cells_of(t_ref, 0, x)
                    new_ref[3, x] = new
                    if x in EDGES:
                        edge_ref[3, EDGES.index(x)] = new

            pltpu.make_async_copy(new_ref.at[f], out_ref.at[f], sems.at[f]).start()

    pl.when(gy == 0)(lambda: run(True))
    pl.when(gy == 1)(lambda: run(False))
    for f in range(8):
        pltpu.make_async_copy(new_ref.at[f], out_ref.at[f], sems.at[f]).wait()


def edge_kernel(t_ref, lo_ref, hi_ref, edge_ref, _, out_ref, new_ref, sems):
    copies = []
    for side in range(2):
        def columns(f, k, side=side):
            if side == 0:
                return lo_ref[f, 16 * k : 16 * k + 16] if k < 2 else cells_of(t_ref, f, k - 2)
            return hi_ref[f, 16 * k - 64 : 16 * k - 48] if k > 3 else cells_of(t_ref, f, k + 12)

        vs = [columns(1, k) / columns(0, k) for k in range(1, 5)]
        faces = [0.5 * (vs[k] + vs[k + 1]) for k in range(3)]
        for f in range(8):
            qs = [columns(f, k) for k in range(6)]
            hs = [0.5 * limited(qs[k] - qs[k - 1], qs[k + 1] - qs[k]) for k in range(1, 5)]
            fluxes = [
                upwind(faces[k], qs[k + 1] + hs[k], qs[k + 2] - hs[k + 1]) for k in range(3)
            ]
            for k in range(2):
                new_ref[side, f, k] = edge_ref[f, 2 * side + k] - DT * (fluxes[k + 1] - fluxes[k])
        copy = pltpu.make_async_copy(
            new_ref.at[side], out_ref.at[:, 14 * side : 14 * side + 2], sems.at[side]
        )
        copy.start()
        copies.append(copy)
    for copy in copies:
        copy.wait()


def local(fields, col_cells, col_num, shear_sub):
    pieces = fields.reshape(NB, 8, 16, 128)
    lines = lax.all_to_all(pieces, "gx", 0, 0, tiled=True)
    send = pl.pallas_call(
        shift_kernel,
        out_shape=jax.ShapeDtypeStruct((NB, 192, 128), jnp.float32),
        in_specs=[SMEM, SMEM, SMEM, VMEM],
        out_specs=VMEM,
        scratch_shapes=[pltpu.VMEM((280, 128), jnp.float32)],
        compiler_params=pltpu.CompilerParams(vmem_limit_bytes=16 * 2**20),
        name="shift",
    )(col_cells, col_num, shear_sub, lines)
    t = lax.all_to_all(send, "gx", 0, 0, tiled=True)
    count = lax.axis_size("gz")
    up = [(i, (i + 1) % count) for i in range(count)]
    down = [(b, a) for a, b in up]
    by_half = t.reshape(8, 2, 192, 128)
    lo = lax.ppermute(by_half[:, 1, 160:], "gz", up)
    hi = lax.ppermute(by_half[:, 0, 160:], "gz", down)
    partner = lax.ppermute(t[:, :128], "gy", [(0, 1), (1, 0)])
    block = jax.ShapeDtypeStruct((8, 16, 16, 128), jnp.float32)
    edges = jax.ShapeDtypeStruct((8, 4, 16, 128), jnp.float32)
    out, edge = pl.pallas_call(
        inner_kernel,
        out_shape=[block, edges],
        in_specs=[VMEM] * 2,
        out_specs=[pl.BlockSpec(memory_space=pl.ANY), VMEM],
        scratch_shapes=[
            pltpu.VMEM((8, 16, 16, 128), jnp.float32),
            pltpu.VMEM((16, 16, 128), jnp.float32),
            pltpu.VMEM((16, 24, 128), jnp.float32),
            pltpu.VMEM((16, 16, 128), jnp.float32),
            pltpu.VMEM((16, 16, 128), jnp.float32),
            pltpu.SemaphoreType.DMA((8,)),
        ],
        compiler_params=pltpu.CompilerParams(vmem_limit_bytes=16 * 2**20),
        cost_estimate=pl.CostEstimate(flops=40_000_000, bytes_accessed=6_000_000, transcendentals=0),
        name="inner",
    )(t, partner)
    return pl.pallas_call(
        edge_kernel,
        out_shape=block,
        in_specs=[VMEM] * 4 + [pl.BlockSpec(memory_space=pl.ANY)],
        out_specs=pl.BlockSpec(memory_space=pl.ANY),
        scratch_shapes=[
            pltpu.VMEM((2, 8, 2, 16, 128), jnp.float32),
            pltpu.SemaphoreType.DMA((2,)),
        ],
        input_output_aliases={4: 0},
        compiler_params=pltpu.CompilerParams(vmem_limit_bytes=16 * 2**20),
        name="edge",
    )(t, lo, hi, edge, out)


def solution(mesh):
    return jax.shard_map(
        local,
        mesh=mesh,
        in_specs=(P(None, "gz", "gx", "gy"), P(), P(), P()),
        out_specs=P(None, "gz", "gx", "gy"),
        check_vma=False,
    )
```

time: 65.3 us -> 63.9 us (0.979)
  Pallas kernels: 7.69 us -> 6.29 us
    pallas_call x3 -> x2, Pallas kernels: 6.39 us -> 4.99 us  [the longest x1 4.1 us: local(): pl.pallas_call(inner_kernel, out_shape=[block, edges], in_specs=[VMEM] *...]
  transfers between devices with their start and end apart: 4 -> 4, of which waited for: 1 -> 1; matrix products, arithmetic and copies ran while one was open for 0% -> 0% of each run, Pallas kernels for 8% -> 6%
where the time goes in v3:
time: 63.9 us; the launch traced here: 63.7 us
  blocking collectives  25.6 us (40%)
  starting transfers between devices  15.7 us (25%)
  waiting for transfers between devices  15.3 us (24%)
  Pallas kernels  6.29 us (10%)
  between operations  0.7 us (1%)
    all_to_all x1, blocking collectives, local(): t = lax.all_to_all(send, 'gx', 0, 0, tiled=True)  25.6 us
    all_to_all x1, waiting for transfers between devices, local(): lines = lax.all_to_all(pieces, 'gx', 0, 0, tiled=True)  15.3 us
    all_to_all x1, starting transfers between devices, local(): lines = lax.all_to_all(pieces, 'gx', 0, 0, tiled=True)  7.72 us
    pallas_call x1, Pallas kernels, local(): pl.pallas_call(inner_kernel, out_shape=[block, edges], in_specs=[VMEM] *...  4.1 us
    ppermute x1, starting transfers between devices, local(): hi = lax.ppermute(by_half[:, 0, 160:], 'gz', down)  4.03 us
    ppermute x1, starting transfers between devices, local(): partner = lax.ppermute(t[:, :128], 'gy', [(0, 1), (1, 0)])  2.21 us
    ppermute x1, starting transfers between devices, local(): lo = lax.ppermute(by_half[:, 1, 160:], 'gz', up)  1.71 us
    pallas_call x1, Pallas kernels, local(): pl.pallas_call(shift_kernel, out_shape=jax.ShapeDtypeStruct((NB, 192, 128...  1.3 us
  transfers between devices with their start and end apart: 4, of which 1 were waited for; matrix products, arithmetic and copies ran while one was open for 0% of the time, Pallas kernels for 6%

profile of v3, /device:TPU:1, one launch (start us, length us, event | category | flops | bytes accessed | tf_op | source)
XLA Modules:
  0.0 63.7 jit_solution(13405331572492953128)
XLA Ops:
  0.0 0.0 copy-start
  0.0 0.0 copy-start.1
  0.0 7.7 %all-to-all-start = ((f32[16,8,16,128]{3,2,1,0:T(8,128)}), f32[16,8,16,128]{3,2,1,0:T(8,128)S(1)}, u32[]{:S(2)}, u32[]{:S(2)}) async-start(f32[16,8,16,128]{3,2,1,0:T(8,128)} %bitcast.11), calls=%async_computation | async-start | bytes 2097152 | tf_op jit(solution)/shard_map/all_to_all | solution.py:219
  8.4 15.3 %all-to-all-done.src_ref = f32[16,8,16,128]{3,2,1,0:T(8,128)S(1)} async-done(((f32[16,8,16,128]{3,2,1,0:T(8,128)}), f32[16,8,16,128]{3,2,1,0:T(8,128)S(1)}, u32[]{:S(2)}, u32[]{:S(2)}) %all-to-all-start) | async-done | bytes 1048608 | tf_op jit(solution)/shard_map/all_to_all | solution.py:219
  23.7 0.0 copy-done
  23.7 0.0 copy-done.1
  23.7 1.3 %shift.1 = f32[16,192,128]{2,1,0:T(8,128)S(1)} custom-call(s32[128]{0:T(128)S(1)} %copy-done, s32[128]{0:T(128)S(1)} %copy-done.1, s32[1]{0:T(128)S(6)} %copy.11.shear_ref, f32[16,8,16,128]{3,2,1,0:T(8,128)S(1)} %all-to-all-done.src_ref), custom_call_target="tpu_custom_call" | custom-call | tf_op jit(solution)/shard_map/shift/pallas_call | solution.py:220
  25.0 25.6 %all_to_all.10.t_ref = f32[16,192,128]{2,1,0:T(8,128)S(1)} all-to-all(f32[16,192,128]{2,1,0:T(8,128)S(1)} %shift.1), channel_id=1, replica_groups=mesh['gx'=16,'gy'=2,'gz'=8] {'gx'}, dimensions={0} | all-to-all | bytes 3145728 | tf_op jit(solution)/shard_map/all_to_all | solution.py:229
  50.6 0.1 slice.14
  50.7 2.2 %collective-permute-start.2 = (f32[16,128,128]{2,1,0:T(8,128)S(1)}, f32[16,128,128]{2,1,0:T(8,128)S(1)}, u32[]{:S(2)}, u32[]{:S(2)}) collective-permute-start(f32[16,128,128]{2,1,0:T(8,128)S(1)} %slice.14), channel_id=1, source_target_pairs={{0,8},{8,0},{1,9},{9,1},{2,10},{10,2},{3,11},{11,3},{4,12},{12,4},... | collective-permute-start | bytes 3145736 | tf_op jit(solution)/shard_map/ppermute | solution.py:236
  53.0 1.7 %collective-permute-start = (f32[8,32,128]{2,1,0:T(8,128)S(1)}, f32[8,32,128]{2,1,0:T(8,128)S(1)}, u32[]{:S(2)}, u32[]{:S(2)}) collective-permute-start(f32[8,32,128]{2,1,0:T(8,128)S(1)} %get-tuple-element.10), channel_id=1, source_target_pairs={{0,1},{1,2},{2,3},{3,4},{4,5},{5,6},{6,7},{7,0},{8,9},{9,10},{10,1... | collective-permute-start | bytes 393224 | tf_op jit(solution)/shard_map/ppermute | solution.py:234
  54.7 4.0 %collective-permute-start.1 = (f32[8,32,128]{2,1,0:T(8,128)S(1)}, f32[8,32,128]{2,1,0:T(8,128)S(1)}, u32[]{:S(2)}, u32[]{:S(2)}) collective-permute-start(f32[8,32,128]{2,1,0:T(8,128)S(1)} %get-tuple-element.9), channel_id=1, source_target_pairs={{1,0},{2,1},{3,2},{4,3},{5,4},{6,5},{7,6},{0,7},{9,8},{10,9},{11,1... | collective-permute-start | bytes 393224 | tf_op jit(solution)/shard_map/ppermute | solution.py:235
  58.7 0.0 collective-permute-done.2.p_ref
  58.7 4.1 %inner.1 = (f32[8,16,16,128]{3,2,1,0:T(8,128)}, f32[8,4,16,128]{3,2,1,0:T(8,128)S(1)}) custom-call(f32[16,192,128]{2,1,0:T(8,128)S(1)} %all_to_all.10.t_ref, f32[16,128,128]{2,1,0:T(8,128)S(1)} %collective-permute-done.2.p_ref), custom_call_target="tpu_custom_call" | custom-call | flops 40000000 | bytes 6000000 | tf_op jit(solution)/shard_map/inner/pallas_call | solution.py:239
  62.8 0.0 collective-permute-done.lo_ref
  62.8 0.0 collective-permute-done.1.hi_ref
  62.8 0.9 %edge.1 = f32[8,16,16,128]{3,2,1,0:T(8,128)} custom-call(f32[16,192,128]{2,1,0:T(8,128)S(1)} %all_to_all.10.t_ref, f32[8,32,128]{2,1,0:T(8,128)S(1)} %collective-permute-done.lo_ref, f32[8,32,128]{2,1,0:T(8,128)S(1)} %collective-permute-done.1.hi_ref, f32[8,4,16,128]{3,2,1,0:T(8,128)S(1)} %get-tuple-element.7.edge_ref, ...), custom_call_target="tpu_custom_call", output_to_operand_aliasing={{}: (4, {})} | custom-call | tf_op jit(solution)/shard_map/edge/pallas_call | solution.py:256
  (1 shorter events, 0.0 us)
Async XLA Ops:
  0.0 23.7 %copy-start = (s32[128]{0:T(128)S(1)}, s32[128]{0:T(128)}, u32[]{:S(2)}) copy-start(s32[128]{0:T(128)} %cells_ref.1) | copy-start | bytes 1540
  0.0 23.7 %copy-start.1 = (s32[128]{0:T(128)S(1)}, s32[128]{0:T(128)}, u32[]{:S(2)}) copy-start(s32[128]{0:T(128)} %num_ref.1) | copy-start | bytes 1540
  0.0 23.7 %all-to-all-start = ((f32[16,8,16,128]{3,2,1,0:T(8,128)}), f32[16,8,16,128]{3,2,1,0:T(8,128)S(1)}, u32[]{:S(2)}, u32[]{:S(2)}) async-start(f32[16,8,16,128]{3,2,1,0:T(8,128)} %bitcast.11), calls=%async_computation | async-start | bytes 2097152 | tf_op jit(solution)/shard_map/all_to_all | solution.py:219
  50.7 8.0 %collective-permute-start.2 = (f32[16,128,128]{2,1,0:T(8,128)S(1)}, f32[16,128,128]{2,1,0:T(8,128)S(1)}, u32[]{:S(2)}, u32[]{:S(2)}) collective-permute-start(f32[16,128,128]{2,1,0:T(8,128)S(1)} %slice.14), channel_id=1, source_target_pairs={{0,8},{8,0},{1,9},{9,1},{2,10},{10,2},{3,11},{11,3},{4,12},{12,4},... | collective-permute-start | bytes 3145736 | tf_op jit(solution)/shard_map/ppermute | solution.py:236
  53.0 9.9 %collective-permute-start = (f32[8,32,128]{2,1,0:T(8,128)S(1)}, f32[8,32,128]{2,1,0:T(8,128)S(1)}, u32[]{:S(2)}, u32[]{:S(2)}) collective-permute-start(f32[8,32,128]{2,1,0:T(8,128)S(1)} %get-tuple-element.10), channel_id=1, source_target_pairs={{0,1},{1,2},{2,3},{3,4},{4,5},{5,6},{6,7},{7,0},{8,9},{9,10},{10,1... | collective-permute-start | bytes 393224 | tf_op jit(solution)/shard_map/ppermute | solution.py:234
  54.7 8.2 %collective-permute-start.1 = (f32[8,32,128]{2,1,0:T(8,128)S(1)}, f32[8,32,128]{2,1,0:T(8,128)S(1)}, u32[]{:S(2)}, u32[]{:S(2)}) collective-permute-start(f32[8,32,128]{2,1,0:T(8,128)S(1)} %get-tuple-element.9), channel_id=1, source_target_pairs={{1,0},{2,1},{3,2},{4,3},{5,4},{6,5},{7,6},{0,7},{9,8},{10,9},{11,1... | collective-permute-start | bytes 393224 | tf_op jit(solution)/shard_map/ppermute | solution.py:235

commit v4 on v3

--- a/solution.py
+++ b/solution.py
@@ -13,7 +13,7 @@
 SMEM = pl.BlockSpec(memory_space=pltpu.SMEM)
 
 
-def shift_kernel(cells_ref, num_ref, shear_ref, src_ref, out_ref, line):
+def shift_kernel(cells_ref, num_ref, shear_ref, src_ref, out_ref, line, total_ref):
     gz = lax.axis_index("gz")
     last = lax.axis_size("gz") - 1
     half = lax.rem(lax.axis_index("gx"), 2)
@@ -22,20 +22,25 @@
     side = jnp.where(
         half == 1, jnp.where(gz == last, shear, 0), jnp.where(gz == 0, -shear, 0)
     )
+    totals = (64 * cells_ref[...] + num_ref[...]).reshape(1, 128).astype(jnp.float32)
+    place = lax.broadcasted_iota(jnp.int32, (1, 128), 1) - first_col
+    for c in range(8):
+        total_ref[c] = jnp.sum(jnp.where(place == c, totals, 0.0)).astype(jnp.int32)
 
     def one(col, extra, row):
-        total = 64 * cells_ref[first_col + col] + num_ref[first_col + col] + extra
+        total = total_ref[col] + extra
         cells = (total >> 6) & 255
         frac = (total & 63).astype(jnp.float32) * (1.0 / 64.0)
+        near = 1.0 - frac
         line[0:8] = src_ref[15, col, 8:16]
         for b in range(16):
             line[8 + 16 * b : 24 + 16 * b] = src_ref[b, col]
         line[264:280] = src_ref[0, col]
-        near = 1.0 - frac
-        for m in range(32):
-            start = ((8 * m - cells) & 255) + 8
-            value = near * line[pl.ds(start, 8)] + frac * line[pl.ds(start - 1, 8)]
-            out_ref[m // 2, pl.ds(pl.multiple_of(row + 8 * (m % 2), 8), 8)] = value
+        for d in range(16):
+            start = ((16 * d - cells) & 255) + 8
+            out_ref[d, pl.ds(pl.multiple_of(row, 16), 16)] = (
+                near * line[pl.ds(start, 16)] + frac * line[pl.ds(start - 1, 16)]
+            )
 
     @pl.loop(0, 8)
     def _(col):
@@ -82,10 +87,7 @@
     return jnp.concatenate([tile, cells_of(t_ref, f, x)], axis=0)
 
 
-EDGES = (0, 1, 14, 15)
-
-
-def inner_kernel(t_ref, p_ref, out_ref, edge_ref, new_ref, ax_ref, ay_ref, lo_ref, hi_ref, sems):
+def inner_kernel(t_ref, p_ref, new_ref, ax_ref, ay_ref, lo_ref, hi_ref):
     gy = lax.axis_index("gy")
     lane = lax.broadcasted_iota(jnp.int32, (16, 128), 1)
     first, final = lane == 0, lane == 127
@@ -144,10 +146,7 @@
             weight = DT * (f == 3).astype(jnp.float32)
 
             def put(x):
-                new = qs[x] - DT * totals[x]
-                new_ref[f, x] = new
-                if x in EDGES:
-                    edge_ref[f, EDGES.index(x)] = new
+                new_ref[f, x] = qs[x] - DT * totals[x]
 
             for x in range(16):
                 ring = ring_of(t_ref, f, x)
@@ -174,21 +173,16 @@
             @pl.when(f == 3)
             def _():
                 for x in range(16):
-                    new = new_ref[3, x] - DT * zc * cells_of(t_ref, 0, x)
-                    new_ref[3, x] = new
-                    if x in EDGES:
-                        edge_ref[3, EDGES.index(x)] = new
-
-            pltpu.make_async_copy(new_ref.at[f], out_ref.at[f], sems.at[f]).start()
+                    new_ref[3, x] = new_ref[3, x] - DT * zc * cells_of(t_ref, 0, x)
 
     pl.when(gy == 0)(lambda: run(True))
     pl.when(gy == 1)(lambda: run(False))
-    for f in range(8):
-        pltpu.make_async_copy(new_ref.at[f], out_ref.at[f], sems.at[f]).wait()
-
-
-def edge_kernel(t_ref, lo_ref, hi_ref, edge_ref, _, out_ref, new_ref, sems):
-    copies = []
+
+
+def edge_kernel(t_ref, lo_ref, hi_ref, new_ref, out_ref, edge_ref, sems):
+    copy = pltpu.make_async_copy(new_ref.at[:, 2:14], out_ref.at[:, 2:14], sems.at[2])
+    copy.start()
+    copies = [copy]
     for side in range(2):
         def columns(f, k, side=side):
             if side == 0:
@@ -204,9 +198,11 @@
                 upwind(faces[k], qs[k + 1] + hs[k], qs[k + 2] - hs[k + 1]) for k in range(3)
             ]
             for k in range(2):
-                new_ref[side, f, k] = edge_ref[f, 2 * side + k] - DT * (fluxes[k + 1] - fluxes[k])
+                edge_ref[side, f, k] = new_ref[f, 14 * side + k] - DT * (
+                    fluxes[k + 1] - fluxes[k]
+                )
         copy = pltpu.make_async_copy(
-            new_ref.at[side], out_ref.at[:, 14 * side : 14 * side + 2], sems.at[side]
+            edge_ref.at[side], out_ref.at[:, 14 * side : 14 * side + 2], sems.at[side]
         )
         copy.start()
         copies.append(copy)
@@ -220,9 +216,9 @@
     send = pl.pallas_call(
         shift_kernel,
         out_shape=jax.ShapeDtypeStruct((NB, 192, 128), jnp.float32),
-        in_specs=[SMEM, SMEM, SMEM, VMEM],
+        in_specs=[VMEM, VMEM, SMEM, VMEM],
         out_specs=VMEM,
-        scratch_shapes=[pltpu.VMEM((280, 128), jnp.float32)],
+        scratch_shapes=[pltpu.VMEM((280, 128), jnp.float32), pltpu.SMEM((8,), jnp.int32)],
         compiler_params=pltpu.CompilerParams(vmem_limit_bytes=16 * 2**20),
         name="shift",
     )(col_cells, col_num, shear_sub, lines)
@@ -235,19 +231,16 @@
     hi = lax.ppermute(by_half[:, 0, 160:], "gz", down)
     partner = lax.ppermute(t[:, :128], "gy", [(0, 1), (1, 0)])
     block = jax.ShapeDtypeStruct((8, 16, 16, 128), jnp.float32)
-    edges = jax.ShapeDtypeStruct((8, 4, 16, 128), jnp.float32)
-    out, edge = pl.pallas_call(
+    new = pl.pallas_call(
         inner_kernel,
-        out_shape=[block, edges],
+        out_shape=block,
         in_specs=[VMEM] * 2,
-        out_specs=[pl.BlockSpec(memory_space=pl.ANY), VMEM],
+        out_specs=VMEM,
         scratch_shapes=[
-            pltpu.VMEM((8, 16, 16, 128), jnp.float32),
             pltpu.VMEM((16, 16, 128), jnp.float32),
             pltpu.VMEM((16, 24, 128), jnp.float32),
             pltpu.VMEM((16, 16, 128), jnp.float32),
             pltpu.VMEM((16, 16, 128), jnp.float32),
-            pltpu.SemaphoreType.DMA((8,)),
         ],
         compiler_params=pltpu.CompilerParams(vmem_limit_bytes=16 * 2**20),
         cost_estimate=pl.CostEstimate(flops=40_000_000, bytes_accessed=6_000_000, transcendentals=0),
@@ -256,16 +249,15 @@
     return pl.pallas_call(
         edge_kernel,
         out_shape=block,
-        in_specs=[VMEM] * 4 + [pl.BlockSpec(memory_space=pl.ANY)],
+        in_specs=[VMEM] * 4,
         out_specs=pl.BlockSpec(memory_space=pl.ANY),
         scratch_shapes=[
             pltpu.VMEM((2, 8, 2, 16, 128), jnp.float32),
-            pltpu.SemaphoreType.DMA((2,)),
+            pltpu.SemaphoreType.DMA((3,)),
         ],
-        input_output_aliases={4: 0},
         compiler_params=pltpu.CompilerParams(vmem_limit_bytes=16 * 2**20),
         name="edge",
-    )(t, lo, hi, edge, out)
+    )(t, lo, hi, new)
 
 
 def solution(mesh):

time: 63.9 us -> 63.1 us (0.987)
  Pallas kernels: 6.29 us -> 5.07 us
    pallas_call x2, Pallas kernels: 4.99 us -> 4.35 us  [the longest x1 3.36 us: local(): pl.pallas_call(inner_kernel, out_shape=block, in_specs=[VMEM] * 2, out_sp...]
  transfers between devices with their start and end apart: 4 -> 4, of which waited for: 1 -> 2; matrix products, arithmetic and copies ran while one was open for 0% -> 0% of each run, Pallas kernels for 6% -> 5%
where the time goes in v4:
time: 63.1 us; the launch traced here: 62.9 us
  blocking collectives  25.6 us (41%)
  starting transfers between devices  15.7 us (25%)
  waiting for transfers between devices  15.7 us (25%)
  Pallas kernels  5.07 us (8%)
  between operations  0.68 us (1%)
    all_to_all x1, blocking collectives, local(): t = lax.all_to_all(send, 'gx', 0, 0, tiled=True)  25.6 us
    all_to_all x1, waiting for transfers between devices, local(): lines = lax.all_to_all(pieces, 'gx', 0, 0, tiled=True)  15.3 us
    all_to_all x1, starting transfers between devices, local(): lines = lax.all_to_all(pieces, 'gx', 0, 0, tiled=True)  7.72 us
    ppermute x1, starting transfers between devices, local(): hi = lax.ppermute(by_half[:, 0, 160:], 'gz', down)  4.03 us
    pallas_call x1, Pallas kernels, local(): pl.pallas_call(inner_kernel, out_shape=block, in_specs=[VMEM] * 2, out_sp...  3.36 us
    ppermute x1, starting transfers between devices, local(): partner = lax.ppermute(t[:, :128], 'gy', [(0, 1), (1, 0)])  2.21 us
    ppermute x1, starting transfers between devices, local(): lo = lax.ppermute(by_half[:, 1, 160:], 'gz', up)  1.71 us
  transfers between devices with their start and end apart: 4, of which 2 were waited for; matrix products, arithmetic and copies ran while one was open for 0% of the time, Pallas kernels for 5%

profile of v4, /device:TPU:1, one launch (start us, length us, event | category | flops | bytes accessed | tf_op | source)
XLA Modules:
  0.0 62.9 jit_solution(7281629426420673668)
XLA Ops:
  0.0 0.0 copy-start
  0.0 0.0 copy-start.1
  0.0 7.7 %all-to-all-start = ((f32[16,8,16,128]{3,2,1,0:T(8,128)}), f32[16,8,16,128]{3,2,1,0:T(8,128)S(1)}, u32[]{:S(2)}, u32[]{:S(2)}) async-start(f32[16,8,16,128]{3,2,1,0:T(8,128)} %bitcast.11), calls=%async_computation | async-start | bytes 2097152 | tf_op jit(solution)/shard_map/all_to_all | solution.py:215
  8.4 15.3 %all-to-all-done.src_ref = f32[16,8,16,128]{3,2,1,0:T(8,128)S(1)} async-done(((f32[16,8,16,128]{3,2,1,0:T(8,128)}), f32[16,8,16,128]{3,2,1,0:T(8,128)S(1)}, u32[]{:S(2)}, u32[]{:S(2)}) %all-to-all-start) | async-done | bytes 1048608 | tf_op jit(solution)/shard_map/all_to_all | solution.py:215
  23.7 0.0 copy-done
  23.7 0.0 copy-done.1
  23.7 0.7 %shift.1 = f32[16,192,128]{2,1,0:T(8,128)S(1)} custom-call(s32[128]{0:T(128)S(1)} %copy-done, s32[128]{0:T(128)S(1)} %copy-done.1, s32[1]{0:T(128)S(6)} %copy.9.shear_ref, f32[16,8,16,128]{3,2,1,0:T(8,128)S(1)} %all-to-all-done.src_ref), custom_call_target="tpu_custom_call" | custom-call | tf_op jit(solution)/shard_map/shift/pallas_call | solution.py:216
  24.4 25.6 %all_to_all.10.t_ref = f32[16,192,128]{2,1,0:T(8,128)S(1)} all-to-all(f32[16,192,128]{2,1,0:T(8,128)S(1)} %shift.1), channel_id=1, replica_groups=mesh['gx'=16,'gy'=2,'gz'=8] {'gx'}, dimensions={0} | all-to-all | bytes 3145728 | tf_op jit(solution)/shard_map/all_to_all | solution.py:225
  50.0 0.1 slice.14
  50.1 2.2 %collective-permute-start.2 = (f32[16,128,128]{2,1,0:T(8,128)S(1)}, f32[16,128,128]{2,1,0:T(8,128)S(1)}, u32[]{:S(2)}, u32[]{:S(2)}) collective-permute-start(f32[16,128,128]{2,1,0:T(8,128)S(1)} %slice.14), channel_id=1, source_target_pairs={{0,8},{8,0},{1,9},{9,1},{2,10},{10,2},{3,11},{11,3},{4,12},{12,4},... | collective-permute-start | bytes 3145736 | tf_op jit(solution)/shard_map/ppermute | solution.py:232
  52.4 1.7 %collective-permute-start = (f32[8,32,128]{2,1,0:T(8,128)S(1)}, f32[8,32,128]{2,1,0:T(8,128)S(1)}, u32[]{:S(2)}, u32[]{:S(2)}) collective-permute-start(f32[8,32,128]{2,1,0:T(8,128)S(1)} %get-tuple-element.6), channel_id=1, source_target_pairs={{0,1},{1,2},{2,3},{3,4},{4,5},{5,6},{6,7},{7,0},{8,9},{9,10},{10,1... | collective-permute-start | bytes 393224 | tf_op jit(solution)/shard_map/ppermute | solution.py:230
  54.1 4.0 %collective-permute-start.1 = (f32[8,32,128]{2,1,0:T(8,128)S(1)}, f32[8,32,128]{2,1,0:T(8,128)S(1)}, u32[]{:S(2)}, u32[]{:S(2)}) collective-permute-start(f32[8,32,128]{2,1,0:T(8,128)S(1)} %get-tuple-element.5), channel_id=1, source_target_pairs={{1,0},{2,1},{3,2},{4,3},{5,4},{6,5},{7,6},{0,7},{9,8},{10,9},{11,1... | collective-permute-start | bytes 393224 | tf_op jit(solution)/shard_map/ppermute | solution.py:231
  58.1 0.0 collective-permute-done.2.p_ref
  58.1 3.4 %inner.1.new_ref = f32[8,16,16,128]{3,2,1,0:T(8,128)S(1)} custom-call(f32[16,192,128]{2,1,0:T(8,128)S(1)} %all_to_all.10.t_ref, f32[16,128,128]{2,1,0:T(8,128)S(1)} %collective-permute-done.2.p_ref), custom_call_target="tpu_custom_call" | custom-call | flops 40000000 | bytes 6000000 | tf_op jit(solution)/shard_map/inner/pallas_call | solution.py:234
  61.5 0.4 collective-permute-done.lo_ref
  61.9 0.0 collective-permute-done.1.hi_ref
  61.9 1.0 %edge.1 = f32[8,16,16,128]{3,2,1,0:T(8,128)} custom-call(f32[16,192,128]{2,1,0:T(8,128)S(1)} %all_to_all.10.t_ref, f32[8,32,128]{2,1,0:T(8,128)S(1)} %collective-permute-done.lo_ref, f32[8,32,128]{2,1,0:T(8,128)S(1)} %collective-permute-done.1.hi_ref, f32[8,16,16,128]{3,2,1,0:T(8,128)S(1)} %inner.1.new_ref), custom_call_target="tpu_custom_call" | custom-call | tf_op jit(solution)/shard_map/edge/pallas_call | solution.py:249
  (1 shorter events, 0.0 us)
Async XLA Ops:
  0.0 23.7 %copy-start = (s32[128]{0:T(128)S(1)}, s32[128]{0:T(128)}, u32[]{:S(2)}) copy-start(s32[128]{0:T(128)} %cells_ref.1) | copy-start | bytes 1540
  0.0 23.7 %copy-start.1 = (s32[128]{0:T(128)S(1)}, s32[128]{0:T(128)}, u32[]{:S(2)}) copy-start(s32[128]{0:T(128)} %num_ref.1) | copy-start | bytes 1540
  0.0 23.7 %all-to-all-start = ((f32[16,8,16,128]{3,2,1,0:T(8,128)}), f32[16,8,16,128]{3,2,1,0:T(8,128)S(1)}, u32[]{:S(2)}, u32[]{:S(2)}) async-start(f32[16,8,16,128]{3,2,1,0:T(8,128)} %bitcast.11), calls=%async_computation | async-start | bytes 2097152 | tf_op jit(solution)/shard_map/all_to_all | solution.py:215
  50.1 8.0 %collective-permute-start.2 = (f32[16,128,128]{2,1,0:T(8,128)S(1)}, f32[16,128,128]{2,1,0:T(8,128)S(1)}, u32[]{:S(2)}, u32[]{:S(2)}) collective-permute-start(f32[16,128,128]{2,1,0:T(8,128)S(1)} %slice.14), channel_id=1, source_target_pairs={{0,8},{8,0},{1,9},{9,1},{2,10},{10,2},{3,11},{11,3},{4,12},{12,4},... | collective-permute-start | bytes 3145736 | tf_op jit(solution)/shard_map/ppermute | solution.py:232
  52.4 9.5 %collective-permute-start = (f32[8,32,128]{2,1,0:T(8,128)S(1)}, f32[8,32,128]{2,1,0:T(8,128)S(1)}, u32[]{:S(2)}, u32[]{:S(2)}) collective-permute-start(f32[8,32,128]{2,1,0:T(8,128)S(1)} %get-tuple-element.6), channel_id=1, source_target_pairs={{0,1},{1,2},{2,3},{3,4},{4,5},{5,6},{6,7},{7,0},{8,9},{9,10},{10,1... | collective-permute-start | bytes 393224 | tf_op jit(solution)/shard_map/ppermute | solution.py:230
  54.1 7.8 %collective-permute-start.1 = (f32[8,32,128]{2,1,0:T(8,128)S(1)}, f32[8,32,128]{2,1,0:T(8,128)S(1)}, u32[]{:S(2)}, u32[]{:S(2)}) collective-permute-start(f32[8,32,128]{2,1,0:T(8,128)S(1)} %get-tuple-element.5), channel_id=1, source_target_pairs={{1,0},{2,1},{3,2},{4,3},{5,4},{6,5},{7,6},{0,7},{9,8},{10,9},{11,1... | collective-permute-start | bytes 393224 | tf_op jit(solution)/shard_map/ppermute | solution.py:231

commit v5 on v4

--- a/solution.py
+++ b/solution.py
@@ -9,6 +9,9 @@
 GRAVITY = 4.0
 NZ = 256
 NB = 16
+ORDER = [9, 0, 2, 12, 11, 7, 8, 14, 10, 1, 13, 15, 3, 6, 5, 4]
+PIECE = [ORDER.index(d) for d in range(NB)]
+UPPER = sum((PIECE[d] % 2) << d for d in range(NB))
 VMEM = pl.BlockSpec(memory_space=pltpu.VMEM)
 SMEM = pl.BlockSpec(memory_space=pltpu.SMEM)
 
@@ -16,7 +19,7 @@
 def shift_kernel(cells_ref, num_ref, shear_ref, src_ref, out_ref, line, total_ref):
     gz = lax.axis_index("gz")
     last = lax.axis_size("gz") - 1
-    half = lax.rem(lax.axis_index("gx"), 2)
+    half = (UPPER >> lax.axis_index("gx")) & 1
     first_col = gz * 16 + half * 8
     shear = shear_ref[0]
     side = jnp.where(
@@ -32,13 +35,13 @@
         cells = (total >> 6) & 255
         frac = (total & 63).astype(jnp.float32) * (1.0 / 64.0)
         near = 1.0 - frac
-        line[0:8] = src_ref[15, col, 8:16]
+        line[0:8] = src_ref[PIECE[15], col, 8:16]
         for b in range(16):
-            line[8 + 16 * b : 24 + 16 * b] = src_ref[b, col]
-        line[264:280] = src_ref[0, col]
+            line[8 + 16 * b : 24 + 16 * b] = src_ref[PIECE[b], col]
+        line[264:280] = src_ref[PIECE[0], col]
         for d in range(16):
             start = ((16 * d - cells) & 255) + 8
-            out_ref[d, pl.ds(pl.multiple_of(row, 16), 16)] = (
+            out_ref[PIECE[d], pl.ds(pl.multiple_of(row, 16), 16)] = (
                 near * line[pl.ds(start, 16)] + frac * line[pl.ds(start - 1, 16)]
             )
 
@@ -57,12 +60,12 @@
     @pl.loop(0, 4)
     def _(c):
         for d in range(16):
-            lo, hi = (d + 15) % 16, (d + 1) % 16
+            lo, hi = PIECE[(d + 15) % 16], PIECE[(d + 1) % 16]
             a = pl.multiple_of(16 * c, 16)
             b = pl.multiple_of(16 * c + 64, 16)
             one_halo = jnp.where(top, out_ref[hi, pl.ds(a, 8)], out_ref[lo, pl.ds(a + 8, 8)])
             two_halo = jnp.where(top, out_ref[hi, pl.ds(b, 8)], out_ref[lo, pl.ds(b + 8, 8)])
-            out_ref[d, pl.ds(pl.multiple_of(128 + 8 * c, 8), 8)] = jnp.where(
+            out_ref[PIECE[d], pl.ds(pl.multiple_of(128 + 8 * c, 8), 8)] = jnp.where(
                 own, one_halo, pltpu.roll(two_halo, 4, 0)
             )
 
@@ -212,7 +215,7 @@
 
 def local(fields, col_cells, col_num, shear_sub):
     pieces = fields.reshape(NB, 8, 16, 128)
-    lines = lax.all_to_all(pieces, "gx", 0, 0, tiled=True)
+    lines = lax.all_to_all(pieces, "gx", 0, 0, tiled=True, axis_index_groups=[ORDER])
     send = pl.pallas_call(
         shift_kernel,
         out_shape=jax.ShapeDtypeStruct((NB, 192, 128), jnp.float32),
@@ -222,7 +225,7 @@
         compiler_params=pltpu.CompilerParams(vmem_limit_bytes=16 * 2**20),
         name="shift",
     )(col_cells, col_num, shear_sub, lines)
-    t = lax.all_to_all(send, "gx", 0, 0, tiled=True)
+    t = lax.all_to_all(send, "gx", 0, 0, tiled=True, axis_index_groups=[ORDER])
     count = lax.axis_size("gz")
     up = [(i, (i + 1) % count) for i in range(count)]
     down = [(b, a) for a, b in up]

time: 63.1 us -> 59.1 us (0.937)
  waiting for transfers between devices: 15.7 us -> 11.3 us
  starting transfers between devices: 15.7 us -> 18.9 us
  blocking collectives: 25.6 us -> 22.7 us
    all_to_all x1, waiting for transfers between devices: 15.3 us -> 10.9 us  [local(): lax.all_to_all(pieces, 'gx', 0, 0, tiled=True, axis_index_groups=[ORDER])]
    all_to_all x1, blocking collectives: 25.6 us -> 22.7 us  [local(): t = lax.all_to_all(send, 'gx', 0, 0, tiled=True, axis_index_groups=[ORDER])]
    ppermute x1, starting transfers between devices: 2.21 us -> 4.51 us  [local(): partner = lax.ppermute(t[:, :128], 'gy', [(0, 1), (1, 0)])]
    all_to_all x1, starting transfers between devices: 7.72 us -> 8.65 us  [local(): lax.all_to_all(pieces, 'gx', 0, 0, tiled=True, axis_index_groups=[ORDER])]
  transfers between devices with their start and end apart: 4 -> 4, of which waited for: 2 -> 2; matrix products, arithmetic and copies ran while one was open for 0% -> 0% of each run, Pallas kernels for 5% -> 6%
where the time goes in v5:
time: 59.1 us; the launch traced here: 58.9 us
  blocking collectives  22.7 us (38%)
  starting transfers between devices  18.9 us (32%)
  waiting for transfers between devices  11.3 us (19%)
  Pallas kernels  5.07 us (9%)
  between operations  0.68 us (1%)
    all_to_all x1, blocking collectives, local(): t = lax.all_to_all(send, 'gx', 0, 0, tiled=True, axis_index_groups=[ORDER])  22.7 us
    all_to_all x1, waiting for transfers between devices, local(): lax.all_to_all(pieces, 'gx', 0, 0, tiled=True, axis_index_groups=[ORDER])  10.9 us
    all_to_all x1, starting transfers between devices, local(): lax.all_to_all(pieces, 'gx', 0, 0, tiled=True, axis_index_groups=[ORDER])  8.65 us
    ppermute x1, starting transfers between devices, local(): partner = lax.ppermute(t[:, :128], 'gy', [(0, 1), (1, 0)])  4.51 us
    ppermute x1, starting transfers between devices, local(): hi = lax.ppermute(by_half[:, 0, 160:], 'gz', down)  4.03 us
    pallas_call x1, Pallas kernels, local(): pl.pallas_call(inner_kernel, out_shape=block, in_specs=[VMEM] * 2, out_sp...  3.36 us
    ppermute x1, starting transfers between devices, local(): lo = lax.ppermute(by_half[:, 1, 160:], 'gz', up)  1.71 us
  transfers between devices with their start and end apart: 4, of which 2 were waited for; matrix products, arithmetic and copies ran while one was open for 0% of the time, Pallas kernels for 6%

profile of v5, /device:TPU:1, one launch (start us, length us, event | category | flops | bytes accessed | tf_op | source)
XLA Modules:
  0.0 58.9 jit_solution(10971239520772356138)
XLA Ops:
  0.0 0.0 copy-start
  0.0 0.0 copy-start.1
  0.0 8.7 %all-to-all-start = ((f32[16,8,16,128]{3,2,1,0:T(8,128)}), f32[16,8,16,128]{3,2,1,0:T(8,128)S(1)}, u32[]{:S(2)}, u32[]{:S(2)}) async-start(f32[16,8,16,128]{3,2,1,0:T(8,128)} %bitcast.11), calls=%async_computation | async-start | bytes 2097152 | tf_op jit(solution)/shard_map/all_to_all | solution.py:218
  9.3 10.9 %all-to-all-done.src_ref = f32[16,8,16,128]{3,2,1,0:T(8,128)S(1)} async-done(((f32[16,8,16,128]{3,2,1,0:T(8,128)}), f32[16,8,16,128]{3,2,1,0:T(8,128)S(1)}, u32[]{:S(2)}, u32[]{:S(2)}) %all-to-all-start) | async-done | bytes 1048608 | tf_op jit(solution)/shard_map/all_to_all | solution.py:218
  20.3 0.0 copy-done
  20.3 0.0 copy-done.1
  20.3 0.7 %shift.1 = f32[16,192,128]{2,1,0:T(8,128)S(1)} custom-call(s32[128]{0:T(128)S(1)} %copy-done, s32[128]{0:T(128)S(1)} %copy-done.1, s32[1]{0:T(128)S(6)} %copy.9.shear_ref, f32[16,8,16,128]{3,2,1,0:T(8,128)S(1)} %all-to-all-done.src_ref), custom_call_target="tpu_custom_call" | custom-call | tf_op jit(solution)/shard_map/shift/pallas_call | solution.py:219
  21.0 22.7 %all_to_all.10.t_ref = f32[16,192,128]{2,1,0:T(8,128)S(1)} all-to-all(f32[16,192,128]{2,1,0:T(8,128)S(1)} %shift.1), channel_id=1, replica_groups={{144,0,32,192,176,112,128,224,160,16,208,240,48,96,80,64},{145,1,33,193..., dimensions={0} | all-to-all | bytes 3145728 | tf_op jit(solution)/shard_map/all_to_all | solution.py:228
  43.7 0.1 slice.14
  43.8 4.5 %collective-permute-start.2 = (f32[16,128,128]{2,1,0:T(8,128)S(1)}, f32[16,128,128]{2,1,0:T(8,128)S(1)}, u32[]{:S(2)}, u32[]{:S(2)}) collective-permute-start(f32[16,128,128]{2,1,0:T(8,128)S(1)} %slice.14), channel_id=1, source_target_pairs={{0,8},{8,0},{1,9},{9,1},{2,10},{10,2},{3,11},{11,3},{4,12},{12,4},... | collective-permute-start | bytes 3145736 | tf_op jit(solution)/shard_map/ppermute | solution.py:235
  48.4 1.7 %collective-permute-start = (f32[8,32,128]{2,1,0:T(8,128)S(1)}, f32[8,32,128]{2,1,0:T(8,128)S(1)}, u32[]{:S(2)}, u32[]{:S(2)}) collective-permute-start(f32[8,32,128]{2,1,0:T(8,128)S(1)} %get-tuple-element.6), channel_id=1, source_target_pairs={{0,1},{1,2},{2,3},{3,4},{4,5},{5,6},{6,7},{7,0},{8,9},{9,10},{10,1... | collective-permute-start | bytes 393224 | tf_op jit(solution)/shard_map/ppermute | solution.py:233
  50.1 4.0 %collective-permute-start.1 = (f32[8,32,128]{2,1,0:T(8,128)S(1)}, f32[8,32,128]{2,1,0:T(8,128)S(1)}, u32[]{:S(2)}, u32[]{:S(2)}) collective-permute-start(f32[8,32,128]{2,1,0:T(8,128)S(1)} %get-tuple-element.5), channel_id=1, source_target_pairs={{1,0},{2,1},{3,2},{4,3},{5,4},{6,5},{7,6},{0,7},{9,8},{10,9},{11,1... | collective-permute-start | bytes 393224 | tf_op jit(solution)/shard_map/ppermute | solution.py:234
  54.1 0.0 collective-permute-done.2.p_ref
  54.1 3.4 %inner.1.new_ref = f32[8,16,16,128]{3,2,1,0:T(8,128)S(1)} custom-call(f32[16,192,128]{2,1,0:T(8,128)S(1)} %all_to_all.10.t_ref, f32[16,128,128]{2,1,0:T(8,128)S(1)} %collective-permute-done.2.p_ref), custom_call_target="tpu_custom_call" | custom-call | flops 40000000 | bytes 6000000 | tf_op jit(solution)/shard_map/inner/pallas_call | solution.py:237
  57.5 0.4 collective-permute-done.lo_ref
  57.9 0.0 collective-permute-done.1.hi_ref
  57.9 1.0 %edge.1 = f32[8,16,16,128]{3,2,1,0:T(8,128)} custom-call(f32[16,192,128]{2,1,0:T(8,128)S(1)} %all_to_all.10.t_ref, f32[8,32,128]{2,1,0:T(8,128)S(1)} %collective-permute-done.lo_ref, f32[8,32,128]{2,1,0:T(8,128)S(1)} %collective-permute-done.1.hi_ref, f32[8,16,16,128]{3,2,1,0:T(8,128)S(1)} %inner.1.new_ref), custom_call_target="tpu_custom_call" | custom-call | tf_op jit(solution)/shard_map/edge/pallas_call | solution.py:252
  (1 shorter events, 0.0 us)
Async XLA Ops:
  0.0 20.3 %copy-start = (s32[128]{0:T(128)S(1)}, s32[128]{0:T(128)}, u32[]{:S(2)}) copy-start(s32[128]{0:T(128)} %cells_ref.1) | copy-start | bytes 1540
  0.0 20.3 %copy-start.1 = (s32[128]{0:T(128)S(1)}, s32[128]{0:T(128)}, u32[]{:S(2)}) copy-start(s32[128]{0:T(128)} %num_ref.1) | copy-start | bytes 1540
  0.0 20.2 %all-to-all-start = ((f32[16,8,16,128]{3,2,1,0:T(8,128)}), f32[16,8,16,128]{3,2,1,0:T(8,128)S(1)}, u32[]{:S(2)}, u32[]{:S(2)}) async-start(f32[16,8,16,128]{3,2,1,0:T(8,128)} %bitcast.11), calls=%async_computation | async-start | bytes 2097152 | tf_op jit(solution)/shard_map/all_to_all | solution.py:218
  43.8 10.3 %collective-permute-start.2 = (f32[16,128,128]{2,1,0:T(8,128)S(1)}, f32[16,128,128]{2,1,0:T(8,128)S(1)}, u32[]{:S(2)}, u32[]{:S(2)}) collective-permute-start(f32[16,128,128]{2,1,0:T(8,128)S(1)} %slice.14), channel_id=1, source_target_pairs={{0,8},{8,0},{1,9},{9,1},{2,10},{10,2},{3,11},{11,3},{4,12},{12,4},... | collective-permute-start | bytes 3145736 | tf_op jit(solution)/shard_map/ppermute | solution.py:235
  48.4 9.5 %collective-permute-start = (f32[8,32,128]{2,1,0:T(8,128)S(1)}, f32[8,32,128]{2,1,0:T(8,128)S(1)}, u32[]{:S(2)}, u32[]{:S(2)}) collective-permute-start(f32[8,32,128]{2,1,0:T(8,128)S(1)} %get-tuple-element.6), channel_id=1, source_target_pairs={{0,1},{1,2},{2,3},{3,4},{4,5},{5,6},{6,7},{7,0},{8,9},{9,10},{10,1... | collective-permute-start | bytes 393224 | tf_op jit(solution)/shard_map/ppermute | solution.py:233
  50.1 7.8 %collective-permute-start.1 = (f32[8,32,128]{2,1,0:T(8,128)S(1)}, f32[8,32,128]{2,1,0:T(8,128)S(1)}, u32[]{:S(2)}, u32[]{:S(2)}) collective-permute-start(f32[8,32,128]{2,1,0:T(8,128)S(1)} %get-tuple-element.5), channel_id=1, source_target_pairs={{1,0},{2,1},{3,2},{4,3},{5,4},{6,5},{7,6},{0,7},{9,8},{10,9},{11,1... | collective-permute-start | bytes 393224 | tf_op jit(solution)/shard_map/ppermute | solution.py:234

commit v6 on v5

--- a/solution.py
+++ b/solution.py
@@ -10,7 +10,10 @@
 NZ = 256
 NB = 16
 ORDER = [9, 0, 2, 12, 11, 7, 8, 14, 10, 1, 13, 15, 3, 6, 5, 4]
+BACK = [9, 0, 2, 12, 1, 15, 8, 14, 10, 11, 13, 7, 3, 6, 5, 4]
 PIECE = [ORDER.index(d) for d in range(NB)]
+SEND = [BACK.index(d) for d in range(NB)]
+SLOT = [BACK.index(d) for d in ORDER]
 UPPER = sum((PIECE[d] % 2) << d for d in range(NB))
 VMEM = pl.BlockSpec(memory_space=pltpu.VMEM)
 SMEM = pl.BlockSpec(memory_space=pltpu.SMEM)
@@ -41,7 +44,7 @@
         line[264:280] = src_ref[PIECE[0], col]
         for d in range(16):
             start = ((16 * d - cells) & 255) + 8
-            out_ref[PIECE[d], pl.ds(pl.multiple_of(row, 16), 16)] = (
+            out_ref[SEND[d], pl.ds(pl.multiple_of(row, 16), 16)] = (
                 near * line[pl.ds(start, 16)] + frac * line[pl.ds(start - 1, 16)]
             )
 
@@ -60,14 +63,21 @@
     @pl.loop(0, 4)
     def _(c):
         for d in range(16):
-            lo, hi = PIECE[(d + 15) % 16], PIECE[(d + 1) % 16]
+            lo, hi = SEND[(d + 15) % 16], SEND[(d + 1) % 16]
             a = pl.multiple_of(16 * c, 16)
             b = pl.multiple_of(16 * c + 64, 16)
             one_halo = jnp.where(top, out_ref[hi, pl.ds(a, 8)], out_ref[lo, pl.ds(a + 8, 8)])
             two_halo = jnp.where(top, out_ref[hi, pl.ds(b, 8)], out_ref[lo, pl.ds(b + 8, 8)])
-            out_ref[PIECE[d], pl.ds(pl.multiple_of(128 + 8 * c, 8), 8)] = jnp.where(
+            out_ref[SEND[d], pl.ds(pl.multiple_of(128 + 8 * c, 8), 8)] = jnp.where(
                 own, one_halo, pltpu.roll(two_halo, 4, 0)
             )
+
+
+def sort_kernel(src_ref, t_ref, cells_ref, up_ref, down_ref):
+    for j in range(NB):
+        t_ref[j] = src_ref[SLOT[j]]
+        cells_ref[j] = src_ref[SLOT[j], :128]
+        (up_ref if j % 2 else down_ref)[j // 2] = src_ref[SLOT[j], 160:]
 
 
 def limited(a, b):
@@ -225,14 +235,27 @@
         compiler_params=pltpu.CompilerParams(vmem_limit_bytes=16 * 2**20),
         name="shift",
     )(col_cells, col_num, shear_sub, lines)
-    t = lax.all_to_all(send, "gx", 0, 0, tiled=True, axis_index_groups=[ORDER])
+    arrived = lax.all_to_all(send, "gx", 0, 0, tiled=True, axis_index_groups=[BACK])
     count = lax.axis_size("gz")
     up = [(i, (i + 1) % count) for i in range(count)]
     down = [(b, a) for a, b in up]
-    by_half = t.reshape(8, 2, 192, 128)
-    lo = lax.ppermute(by_half[:, 1, 160:], "gz", up)
-    hi = lax.ppermute(by_half[:, 0, 160:], "gz", down)
-    partner = lax.ppermute(t[:, :128], "gy", [(0, 1), (1, 0)])
+    column = jax.ShapeDtypeStruct((8, 32, 128), jnp.float32)
+    t, cells, upper, lower = pl.pallas_call(
+        sort_kernel,
+        out_shape=[
+            jax.ShapeDtypeStruct((NB, 192, 128), jnp.float32),
+            jax.ShapeDtypeStruct((NB, 128, 128), jnp.float32),
+            column,
+            column,
+        ],
+        in_specs=[VMEM],
+        out_specs=[VMEM] * 4,
+        compiler_params=pltpu.CompilerParams(vmem_limit_bytes=16 * 2**20),
+        name="sort",
+    )(arrived)
+    lo = lax.ppermute(upper, "gz", up)
+    hi = lax.ppermute(lower, "gz", down)
+    partner = lax.ppermute(cells, "gy", [(0, 1), (1, 0)])
     block = jax.ShapeDtypeStruct((8, 16, 16, 128), jnp.float32)
     new = pl.pallas_call(
         inner_kernel,

time: 59.1 us -> 59.2 us (level)
  blocking collectives: 22.7 us -> 23.3 us
where the time goes in v6:
time: 59.2 us; the launch traced here: 59 us
  blocking collectives  23.3 us (39%)
  starting transfers between devices  18.4 us (31%)
  waiting for transfers between devices  11.4 us (19%)
  Pallas kernels  5.25 us (9%)
  between operations  0.67 us (1%)
    all_to_all x1, blocking collectives, local(): lax.all_to_all(send, 'gx', 0, 0, tiled=True, axis_index_groups=[BACK])  23.3 us
    all_to_all x1, waiting for transfers between devices, local(): lax.all_to_all(pieces, 'gx', 0, 0, tiled=True, axis_index_groups=[ORDER])  10.9 us
    all_to_all x1, starting transfers between devices, local(): lax.all_to_all(pieces, 'gx', 0, 0, tiled=True, axis_index_groups=[ORDER])  8.65 us
    ppermute x1, starting transfers between devices, local(): partner = lax.ppermute(cells, 'gy', [(0, 1), (1, 0)])  4.19 us
    ppermute x1, starting transfers between devices, local(): hi = lax.ppermute(lower, 'gz', down)  3.93 us
    pallas_call x1, Pallas kernels, local(): pl.pallas_call(inner_kernel, out_shape=block, in_specs=[VMEM] * 2, out_sp...  3.36 us
    ppermute x1, starting transfers between devices, local(): lo = lax.ppermute(upper, 'gz', up)  1.65 us
  transfers between devices with their start and end apart: 4, of which 2 were waited for; matrix products, arithmetic and copies ran while one was open for 0% of the time, Pallas kernels for 6%

profile of v6, /device:TPU:1, one launch (start us, length us, event | category | flops | bytes accessed | tf_op | source)
XLA Modules:
  0.0 59.0 jit_solution(14641522218930628360)
XLA Ops:
  0.0 0.0 copy-start.1
  0.0 0.0 copy-start
  0.0 8.7 %all-to-all-start = ((f32[16,8,16,128]{3,2,1,0:T(8,128)}), f32[16,8,16,128]{3,2,1,0:T(8,128)S(1)}, u32[]{:S(2)}, u32[]{:S(2)}) async-start(f32[16,8,16,128]{3,2,1,0:T(8,128)} %bitcast.1), calls=%async_computation | async-start | bytes 2097152 | tf_op jit(solution)/shard_map/all_to_all | solution.py:228
  9.3 10.9 %all-to-all-done.src_ref = f32[16,8,16,128]{3,2,1,0:T(8,128)S(1)} async-done(((f32[16,8,16,128]{3,2,1,0:T(8,128)}), f32[16,8,16,128]{3,2,1,0:T(8,128)S(1)}, u32[]{:S(2)}, u32[]{:S(2)}) %all-to-all-start) | async-done | bytes 1048608 | tf_op jit(solution)/shard_map/all_to_all | solution.py:228
  20.3 0.0 copy-done.1
  20.3 0.0 copy-done
  20.3 0.7 %shift.1 = f32[16,192,128]{2,1,0:T(8,128)S(1)} custom-call(s32[128]{0:T(128)S(1)} %copy-done, s32[128]{0:T(128)S(1)} %copy-done.1, s32[1]{0:T(128)S(6)} %copy.5.shear_ref, f32[16,8,16,128]{3,2,1,0:T(8,128)S(1)} %all-to-all-done.src_ref), custom_call_target="tpu_custom_call" | custom-call | tf_op jit(solution)/shard_map/shift/pallas_call | solution.py:229
  21.0 23.3 %all_to_all.10.src_ref = f32[16,192,128]{2,1,0:T(8,128)S(1)} all-to-all(f32[16,192,128]{2,1,0:T(8,128)S(1)} %shift.1), channel_id=1, replica_groups={{144,0,32,192,16,240,128,224,160,176,208,112,48,96,80,64},{145,1,33,193..., dimensions={0} | all-to-all | bytes 3145728 | tf_op jit(solution)/shard_map/all_to_all | solution.py:238
  44.2 0.2 sort.1
  44.4 4.2 %collective-permute-start.2 = (f32[16,128,128]{2,1,0:T(8,128)S(1)}, f32[16,128,128]{2,1,0:T(8,128)S(1)}, u32[]{:S(2)}, u32[]{:S(2)}) collective-permute-start(f32[16,128,128]{2,1,0:T(8,128)S(1)} %get-tuple-element.12), channel_id=1, source_target_pairs={{0,8},{8,0},{1,9},{9,1},{2,10},{10,2},{3,11},{11,3},{4,12},{12,4},... | collective-permute-start | bytes 3145736 | tf_op jit(solution)/shard_map/ppermute | solution.py:258
  48.6 1.6 %collective-permute-start = (f32[8,32,128]{2,1,0:T(8,128)S(1)}, f32[8,32,128]{2,1,0:T(8,128)S(1)}, u32[]{:S(2)}, u32[]{:S(2)}) collective-permute-start(f32[8,32,128]{2,1,0:T(8,128)S(1)} %get-tuple-element.10), channel_id=1, source_target_pairs={{0,1},{1,2},{2,3},{3,4},{4,5},{5,6},{6,7},{7,0},{8,9},{9,10},{10,1... | collective-permute-start | bytes 393224 | tf_op jit(solution)/shard_map/ppermute | solution.py:256
  50.3 3.9 %collective-permute-start.1 = (f32[8,32,128]{2,1,0:T(8,128)S(1)}, f32[8,32,128]{2,1,0:T(8,128)S(1)}, u32[]{:S(2)}, u32[]{:S(2)}) collective-permute-start(f32[8,32,128]{2,1,0:T(8,128)S(1)} %get-tuple-element.11), channel_id=1, source_target_pairs={{1,0},{2,1},{3,2},{4,3},{5,4},{6,5},{7,6},{0,7},{9,8},{10,9},{11,1... | collective-permute-start | bytes 393224 | tf_op jit(solution)/shard_map/ppermute | solution.py:257
  54.2 0.0 collective-permute-done.2.p_ref
  54.2 3.4 %inner.1.new_ref = f32[8,16,16,128]{3,2,1,0:T(8,128)S(1)} custom-call(f32[16,192,128]{2,1,0:T(8,128)S(1)} %get-tuple-element.9.t_ref, f32[16,128,128]{2,1,0:T(8,128)S(1)} %collective-permute-done.2.p_ref), custom_call_target="tpu_custom_call" | custom-call | flops 40000000 | bytes 6000000 | tf_op jit(solution)/shard_map/inner/pallas_call | solution.py:260
  57.6 0.4 collective-permute-done.lo_ref
  58.0 0.0 collective-permute-done.1.hi_ref
  58.0 1.0 %edge.1 = f32[8,16,16,128]{3,2,1,0:T(8,128)} custom-call(f32[16,192,128]{2,1,0:T(8,128)S(1)} %get-tuple-element.9.t_ref, f32[8,32,128]{2,1,0:T(8,128)S(1)} %collective-permute-done.lo_ref, f32[8,32,128]{2,1,0:T(8,128)S(1)} %collective-permute-done.1.hi_ref, f32[8,16,16,128]{3,2,1,0:T(8,128)S(1)} %inner.1.new_ref), custom_call_target="tpu_custom_call" | custom-call | tf_op jit(solution)/shard_map/edge/pallas_call | solution.py:275
Async XLA Ops:
  0.0 20.3 %copy-start.1 = (s32[128]{0:T(128)S(1)}, s32[128]{0:T(128)}, u32[]{:S(2)}) copy-start(s32[128]{0:T(128)} %num_ref.1) | copy-start | bytes 1540
  0.0 20.3 %copy-start = (s32[128]{0:T(128)S(1)}, s32[128]{0:T(128)}, u32[]{:S(2)}) copy-start(s32[128]{0:T(128)} %cells_ref.1) | copy-start | bytes 1540
  0.0 20.2 %all-to-all-start = ((f32[16,8,16,128]{3,2,1,0:T(8,128)}), f32[16,8,16,128]{3,2,1,0:T(8,128)S(1)}, u32[]{:S(2)}, u32[]{:S(2)}) async-start(f32[16,8,16,128]{3,2,1,0:T(8,128)} %bitcast.1), calls=%async_computation | async-start | bytes 2097152 | tf_op jit(solution)/shard_map/all_to_all | solution.py:228
  44.4 9.8 %collective-permute-start.2 = (f32[16,128,128]{2,1,0:T(8,128)S(1)}, f32[16,128,128]{2,1,0:T(8,128)S(1)}, u32[]{:S(2)}, u32[]{:S(2)}) collective-permute-start(f32[16,128,128]{2,1,0:T(8,128)S(1)} %get-tuple-element.12), channel_id=1, source_target_pairs={{0,8},{8,0},{1,9},{9,1},{2,10},{10,2},{3,11},{11,3},{4,12},{12,4},... | collective-permute-start | bytes 3145736 | tf_op jit(solution)/shard_map/ppermute | solution.py:258
  48.6 9.4 %collective-permute-start = (f32[8,32,128]{2,1,0:T(8,128)S(1)}, f32[8,32,128]{2,1,0:T(8,128)S(1)}, u32[]{:S(2)}, u32[]{:S(2)}) collective-permute-start(f32[8,32,128]{2,1,0:T(8,128)S(1)} %get-tuple-element.10), channel_id=1, source_target_pairs={{0,1},{1,2},{2,3},{3,4},{4,5},{5,6},{6,7},{7,0},{8,9},{9,10},{10,1... | collective-permute-start | bytes 393224 | tf_op jit(solution)/shard_map/ppermute | solution.py:256
  50.3 7.7 %collective-permute-start.1 = (f32[8,32,128]{2,1,0:T(8,128)S(1)}, f32[8,32,128]{2,1,0:T(8,128)S(1)}, u32[]{:S(2)}, u32[]{:S(2)}) collective-permute-start(f32[8,32,128]{2,1,0:T(8,128)S(1)} %get-tuple-element.11), channel_id=1, source_target_pairs={{1,0},{2,1},{3,2},{4,3},{5,4},{6,5},{7,6},{0,7},{9,8},{10,9},{11,1... | collective-permute-start | bytes 393224 | tf_op jit(solution)/shard_map/ppermute | solution.py:257

commit v7 on v5

--- a/solution.py
+++ b/solution.py
@@ -57,7 +57,7 @@
     top = sub < 4
     own = (sub < 2) | (sub >= 6)
 
-    @pl.loop(0, 4)
+    @pl.loop(0, 4, unroll=4)
     def _(c):
         for d in range(16):
             lo, hi = PIECE[(d + 15) % 16], PIECE[(d + 1) % 16]

time: 59.1 us -> 58.9 us (level)
  no operation moved by 1% of the time
where the time goes in v7:
time: 58.9 us; the launch traced here: 58.7 us
  blocking collectives  22.7 us (39%)
  starting transfers between devices  18.9 us (32%)
  waiting for transfers between devices  11.3 us (19%)
  Pallas kernels  4.89 us (8%)
  between operations  0.69 us (1%)
    all_to_all x1, blocking collectives, local(): t = lax.all_to_all(send, 'gx', 0, 0, tiled=True, axis_index_groups=[ORDER])  22.7 us
    all_to_all x1, waiting for transfers between devices, local(): lax.all_to_all(pieces, 'gx', 0, 0, tiled=True, axis_index_groups=[ORDER])  10.9 us
    all_to_all x1, starting transfers between devices, local(): lax.all_to_all(pieces, 'gx', 0, 0, tiled=True, axis_index_groups=[ORDER])  8.65 us
    ppermute x1, starting transfers between devices, local(): partner = lax.ppermute(t[:, :128], 'gy', [(0, 1), (1, 0)])  4.51 us
    ppermute x1, starting transfers between devices, local(): hi = lax.ppermute(by_half[:, 0, 160:], 'gz', down)  4.03 us
    pallas_call x1, Pallas kernels, local(): pl.pallas_call(inner_kernel, out_shape=block, in_specs=[VMEM] * 2, out_sp...  3.36 us
    ppermute x1, starting transfers between devices, local(): lo = lax.ppermute(by_half[:, 1, 160:], 'gz', up)  1.71 us
  transfers between devices with their start and end apart: 4, of which 2 were waited for; matrix products, arithmetic and copies ran while one was open for 0% of the time, Pallas kernels for 6%

profile of v7, /device:TPU:1, one launch (start us, length us, event | category | flops | bytes accessed | tf_op | source)
XLA Modules:
  0.0 58.7 jit_solution(4503157336118224005)
XLA Ops:
  0.0 0.0 copy-start
  0.0 0.0 copy-start.1
  0.0 8.7 %all-to-all-start = ((f32[16,8,16,128]{3,2,1,0:T(8,128)}), f32[16,8,16,128]{3,2,1,0:T(8,128)S(1)}, u32[]{:S(2)}, u32[]{:S(2)}) async-start(f32[16,8,16,128]{3,2,1,0:T(8,128)} %bitcast.11), calls=%async_computation | async-start | bytes 2097152 | tf_op jit(solution)/shard_map/all_to_all | solution.py:218
  9.3 10.9 %all-to-all-done.src_ref = f32[16,8,16,128]{3,2,1,0:T(8,128)S(1)} async-done(((f32[16,8,16,128]{3,2,1,0:T(8,128)}), f32[16,8,16,128]{3,2,1,0:T(8,128)S(1)}, u32[]{:S(2)}, u32[]{:S(2)}) %all-to-all-start) | async-done | bytes 1048608 | tf_op jit(solution)/shard_map/all_to_all | solution.py:218
  20.3 0.0 copy-done
  20.3 0.0 copy-done.1
  20.3 0.5 shift.1
  20.8 22.7 %all_to_all.10.t_ref = f32[16,192,128]{2,1,0:T(8,128)S(1)} all-to-all(f32[16,192,128]{2,1,0:T(8,128)S(1)} %shift.1), channel_id=1, replica_groups={{144,0,32,192,176,112,128,224,160,16,208,240,48,96,80,64},{145,1,33,193..., dimensions={0} | all-to-all | bytes 3145728 | tf_op jit(solution)/shard_map/all_to_all | solution.py:228
  43.5 0.1 slice.14
  43.6 4.5 %collective-permute-start.2 = (f32[16,128,128]{2,1,0:T(8,128)S(1)}, f32[16,128,128]{2,1,0:T(8,128)S(1)}, u32[]{:S(2)}, u32[]{:S(2)}) collective-permute-start(f32[16,128,128]{2,1,0:T(8,128)S(1)} %slice.14), channel_id=1, source_target_pairs={{0,8},{8,0},{1,9},{9,1},{2,10},{10,2},{3,11},{11,3},{4,12},{12,4},... | collective-permute-start | bytes 3145736 | tf_op jit(solution)/shard_map/ppermute | solution.py:235
  48.2 1.7 %collective-permute-start = (f32[8,32,128]{2,1,0:T(8,128)S(1)}, f32[8,32,128]{2,1,0:T(8,128)S(1)}, u32[]{:S(2)}, u32[]{:S(2)}) collective-permute-start(f32[8,32,128]{2,1,0:T(8,128)S(1)} %get-tuple-element.6), channel_id=1, source_target_pairs={{0,1},{1,2},{2,3},{3,4},{4,5},{5,6},{6,7},{7,0},{8,9},{9,10},{10,1... | collective-permute-start | bytes 393224 | tf_op jit(solution)/shard_map/ppermute | solution.py:233
  49.9 4.0 %collective-permute-start.1 = (f32[8,32,128]{2,1,0:T(8,128)S(1)}, f32[8,32,128]{2,1,0:T(8,128)S(1)}, u32[]{:S(2)}, u32[]{:S(2)}) collective-permute-start(f32[8,32,128]{2,1,0:T(8,128)S(1)} %get-tuple-element.5), channel_id=1, source_target_pairs={{1,0},{2,1},{3,2},{4,3},{5,4},{6,5},{7,6},{0,7},{9,8},{10,9},{11,1... | collective-permute-start | bytes 393224 | tf_op jit(solution)/shard_map/ppermute | solution.py:234
  53.9 0.0 collective-permute-done.2.p_ref
  53.9 3.4 %inner.1.new_ref = f32[8,16,16,128]{3,2,1,0:T(8,128)S(1)} custom-call(f32[16,192,128]{2,1,0:T(8,128)S(1)} %all_to_all.10.t_ref, f32[16,128,128]{2,1,0:T(8,128)S(1)} %collective-permute-done.2.p_ref), custom_call_target="tpu_custom_call" | custom-call | flops 40000000 | bytes 6000000 | tf_op jit(solution)/shard_map/inner/pallas_call | solution.py:237
  57.3 0.4 collective-permute-done.lo_ref
  57.7 0.0 collective-permute-done.1.hi_ref
  57.7 1.0 %edge.1 = f32[8,16,16,128]{3,2,1,0:T(8,128)} custom-call(f32[16,192,128]{2,1,0:T(8,128)S(1)} %all_to_all.10.t_ref, f32[8,32,128]{2,1,0:T(8,128)S(1)} %collective-permute-done.lo_ref, f32[8,32,128]{2,1,0:T(8,128)S(1)} %collective-permute-done.1.hi_ref, f32[8,16,16,128]{3,2,1,0:T(8,128)S(1)} %inner.1.new_ref), custom_call_target="tpu_custom_call" | custom-call | tf_op jit(solution)/shard_map/edge/pallas_call | solution.py:252
  (1 shorter events, 0.0 us)
Async XLA Ops:
  0.0 20.3 %copy-start = (s32[128]{0:T(128)S(1)}, s32[128]{0:T(128)}, u32[]{:S(2)}) copy-start(s32[128]{0:T(128)} %cells_ref.1) | copy-start | bytes 1540
  0.0 20.3 %copy-start.1 = (s32[128]{0:T(128)S(1)}, s32[128]{0:T(128)}, u32[]{:S(2)}) copy-start(s32[128]{0:T(128)} %num_ref.1) | copy-start | bytes 1540
  0.0 20.2 %all-to-all-start = ((f32[16,8,16,128]{3,2,1,0:T(8,128)}), f32[16,8,16,128]{3,2,1,0:T(8,128)S(1)}, u32[]{:S(2)}, u32[]{:S(2)}) async-start(f32[16,8,16,128]{3,2,1,0:T(8,128)} %bitcast.11), calls=%async_computation | async-start | bytes 2097152 | tf_op jit(solution)/shard_map/all_to_all | solution.py:218
  43.6 10.3 %collective-permute-start.2 = (f32[16,128,128]{2,1,0:T(8,128)S(1)}, f32[16,128,128]{2,1,0:T(8,128)S(1)}, u32[]{:S(2)}, u32[]{:S(2)}) collective-permute-start(f32[16,128,128]{2,1,0:T(8,128)S(1)} %slice.14), channel_id=1, source_target_pairs={{0,8},{8,0},{1,9},{9,1},{2,10},{10,2},{3,11},{11,3},{4,12},{12,4},... | collective-permute-start | bytes 3145736 | tf_op jit(solution)/shard_map/ppermute | solution.py:235
  48.2 9.5 %collective-permute-start = (f32[8,32,128]{2,1,0:T(8,128)S(1)}, f32[8,32,128]{2,1,0:T(8,128)S(1)}, u32[]{:S(2)}, u32[]{:S(2)}) collective-permute-start(f32[8,32,128]{2,1,0:T(8,128)S(1)} %get-tuple-element.6), channel_id=1, source_target_pairs={{0,1},{1,2},{2,3},{3,4},{4,5},{5,6},{6,7},{7,0},{8,9},{9,10},{10,1... | collective-permute-start | bytes 393224 | tf_op jit(solution)/shard_map/ppermute | solution.py:233
  49.9 7.8 %collective-permute-start.1 = (f32[8,32,128]{2,1,0:T(8,128)S(1)}, f32[8,32,128]{2,1,0:T(8,128)S(1)}, u32[]{:S(2)}, u32[]{:S(2)}) collective-permute-start(f32[8,32,128]{2,1,0:T(8,128)S(1)} %get-tuple-element.5), channel_id=1, source_target_pairs={{1,0},{2,1},{3,2},{4,3},{5,4},{6,5},{7,6},{0,7},{9,8},{10,9},{11,1... | collective-permute-start | bytes 393224 | tf_op jit(solution)/shard_map/ppermute | solution.py:234

commit v8 on v7

--- a/solution.py
+++ b/solution.py
@@ -49,7 +49,7 @@
     def _(col):
         one(col, 0, 16 * col)
 
-    @pl.loop(0, 2)
+    @pl.loop(0, 2, unroll=2)
     def _(e):
         one(e + 6 * half, side, 160 + 16 * e)
 

time: 58.9 us -> 58.9 us (level)
  no operation moved by 1% of the time
where the time goes in v8:
time: 58.9 us; the launch traced here: 58.7 us
  blocking collectives  22.7 us (39%)
  starting transfers between devices  18.9 us (32%)
  waiting for transfers between devices  11.3 us (19%)
  Pallas kernels  4.89 us (8%)
  between operations  0.68 us (1%)
    all_to_all x1, blocking collectives, local(): t = lax.all_to_all(send, 'gx', 0, 0, tiled=True, axis_index_groups=[ORDER])  22.7 us
    all_to_all x1, waiting for transfers between devices, local(): lax.all_to_all(pieces, 'gx', 0, 0, tiled=True, axis_index_groups=[ORDER])  10.9 us
    all_to_all x1, starting transfers between devices, local(): lax.all_to_all(pieces, 'gx', 0, 0, tiled=True, axis_index_groups=[ORDER])  8.65 us
    ppermute x1, starting transfers between devices, local(): partner = lax.ppermute(t[:, :128], 'gy', [(0, 1), (1, 0)])  4.51 us
    ppermute x1, starting transfers between devices, local(): hi = lax.ppermute(by_half[:, 0, 160:], 'gz', down)  4.03 us
    pallas_call x1, Pallas kernels, local(): pl.pallas_call(inner_kernel, out_shape=block, in_specs=[VMEM] * 2, out_sp...  3.36 us
    ppermute x1, starting transfers between devices, local(): lo = lax.ppermute(by_half[:, 1, 160:], 'gz', up)  1.71 us
  transfers between devices with their start and end apart: 4, of which 2 were waited for; matrix products, arithmetic and copies ran while one was open for 0% of the time, Pallas kernels for 6%

profile of v8, /device:TPU:1, one launch (start us, length us, event | category | flops | bytes accessed | tf_op | source)
XLA Modules:
  0.0 58.7 jit_solution(10353715343107937718)
XLA Ops:
  0.0 0.0 copy-start
  0.0 0.0 copy-start.1
  0.0 8.7 %all-to-all-start = ((f32[16,8,16,128]{3,2,1,0:T(8,128)}), f32[16,8,16,128]{3,2,1,0:T(8,128)S(1)}, u32[]{:S(2)}, u32[]{:S(2)}) async-start(f32[16,8,16,128]{3,2,1,0:T(8,128)} %bitcast.11), calls=%async_computation | async-start | bytes 2097152 | tf_op jit(solution)/shard_map/all_to_all | solution.py:218
  9.3 10.9 %all-to-all-done.src_ref = f32[16,8,16,128]{3,2,1,0:T(8,128)S(1)} async-done(((f32[16,8,16,128]{3,2,1,0:T(8,128)}), f32[16,8,16,128]{3,2,1,0:T(8,128)S(1)}, u32[]{:S(2)}, u32[]{:S(2)}) %all-to-all-start) | async-done | bytes 1048608 | tf_op jit(solution)/shard_map/all_to_all | solution.py:218
  20.3 0.0 copy-done
  20.3 0.0 copy-done.1
  20.3 0.5 shift.1
  20.8 22.7 %all_to_all.10.t_ref = f32[16,192,128]{2,1,0:T(8,128)S(1)} all-to-all(f32[16,192,128]{2,1,0:T(8,128)S(1)} %shift.1), channel_id=1, replica_groups={{144,0,32,192,176,112,128,224,160,16,208,240,48,96,80,64},{145,1,33,193..., dimensions={0} | all-to-all | bytes 3145728 | tf_op jit(solution)/shard_map/all_to_all | solution.py:228
  43.5 0.1 slice.14
  43.6 4.5 %collective-permute-start.2 = (f32[16,128,128]{2,1,0:T(8,128)S(1)}, f32[16,128,128]{2,1,0:T(8,128)S(1)}, u32[]{:S(2)}, u32[]{:S(2)}) collective-permute-start(f32[16,128,128]{2,1,0:T(8,128)S(1)} %slice.14), channel_id=1, source_target_pairs={{0,8},{8,0},{1,9},{9,1},{2,10},{10,2},{3,11},{11,3},{4,12},{12,4},... | collective-permute-start | bytes 3145736 | tf_op jit(solution)/shard_map/ppermute | solution.py:235
  48.2 1.7 %collective-permute-start = (f32[8,32,128]{2,1,0:T(8,128)S(1)}, f32[8,32,128]{2,1,0:T(8,128)S(1)}, u32[]{:S(2)}, u32[]{:S(2)}) collective-permute-start(f32[8,32,128]{2,1,0:T(8,128)S(1)} %get-tuple-element.6), channel_id=1, source_target_pairs={{0,1},{1,2},{2,3},{3,4},{4,5},{5,6},{6,7},{7,0},{8,9},{9,10},{10,1... | collective-permute-start | bytes 393224 | tf_op jit(solution)/shard_map/ppermute | solution.py:233
  49.9 4.0 %collective-permute-start.1 = (f32[8,32,128]{2,1,0:T(8,128)S(1)}, f32[8,32,128]{2,1,0:T(8,128)S(1)}, u32[]{:S(2)}, u32[]{:S(2)}) collective-permute-start(f32[8,32,128]{2,1,0:T(8,128)S(1)} %get-tuple-element.5), channel_id=1, source_target_pairs={{1,0},{2,1},{3,2},{4,3},{5,4},{6,5},{7,6},{0,7},{9,8},{10,9},{11,1... | collective-permute-start | bytes 393224 | tf_op jit(solution)/shard_map/ppermute | solution.py:234
  53.9 0.0 collective-permute-done.2.p_ref
  53.9 3.4 %inner.1.new_ref = f32[8,16,16,128]{3,2,1,0:T(8,128)S(1)} custom-call(f32[16,192,128]{2,1,0:T(8,128)S(1)} %all_to_all.10.t_ref, f32[16,128,128]{2,1,0:T(8,128)S(1)} %collective-permute-done.2.p_ref), custom_call_target="tpu_custom_call" | custom-call | flops 40000000 | bytes 6000000 | tf_op jit(solution)/shard_map/inner/pallas_call | solution.py:237
  57.3 0.4 collective-permute-done.lo_ref
  57.7 0.0 collective-permute-done.1.hi_ref
  57.7 1.0 %edge.1 = f32[8,16,16,128]{3,2,1,0:T(8,128)} custom-call(f32[16,192,128]{2,1,0:T(8,128)S(1)} %all_to_all.10.t_ref, f32[8,32,128]{2,1,0:T(8,128)S(1)} %collective-permute-done.lo_ref, f32[8,32,128]{2,1,0:T(8,128)S(1)} %collective-permute-done.1.hi_ref, f32[8,16,16,128]{3,2,1,0:T(8,128)S(1)} %inner.1.new_ref), custom_call_target="tpu_custom_call" | custom-call | tf_op jit(solution)/shard_map/edge/pallas_call | solution.py:252
  (1 shorter events, 0.0 us)
Async XLA Ops:
  0.0 20.3 %copy-start = (s32[128]{0:T(128)S(1)}, s32[128]{0:T(128)}, u32[]{:S(2)}) copy-start(s32[128]{0:T(128)} %cells_ref.1) | copy-start | bytes 1540
  0.0 20.3 %copy-start.1 = (s32[128]{0:T(128)S(1)}, s32[128]{0:T(128)}, u32[]{:S(2)}) copy-start(s32[128]{0:T(128)} %num_ref.1) | copy-start | bytes 1540
  0.0 20.2 %all-to-all-start = ((f32[16,8,16,128]{3,2,1,0:T(8,128)}), f32[16,8,16,128]{3,2,1,0:T(8,128)S(1)}, u32[]{:S(2)}, u32[]{:S(2)}) async-start(f32[16,8,16,128]{3,2,1,0:T(8,128)} %bitcast.11), calls=%async_computation | async-start | bytes 2097152 | tf_op jit(solution)/shard_map/all_to_all | solution.py:218
  43.6 10.3 %collective-permute-start.2 = (f32[16,128,128]{2,1,0:T(8,128)S(1)}, f32[16,128,128]{2,1,0:T(8,128)S(1)}, u32[]{:S(2)}, u32[]{:S(2)}) collective-permute-start(f32[16,128,128]{2,1,0:T(8,128)S(1)} %slice.14), channel_id=1, source_target_pairs={{0,8},{8,0},{1,9},{9,1},{2,10},{10,2},{3,11},{11,3},{4,12},{12,4},... | collective-permute-start | bytes 3145736 | tf_op jit(solution)/shard_map/ppermute | solution.py:235
  48.2 9.5 %collective-permute-start = (f32[8,32,128]{2,1,0:T(8,128)S(1)}, f32[8,32,128]{2,1,0:T(8,128)S(1)}, u32[]{:S(2)}, u32[]{:S(2)}) collective-permute-start(f32[8,32,128]{2,1,0:T(8,128)S(1)} %get-tuple-element.6), channel_id=1, source_target_pairs={{0,1},{1,2},{2,3},{3,4},{4,5},{5,6},{6,7},{7,0},{8,9},{9,10},{10,1... | collective-permute-start | bytes 393224 | tf_op jit(solution)/shard_map/ppermute | solution.py:233
  49.9 7.8 %collective-permute-start.1 = (f32[8,32,128]{2,1,0:T(8,128)S(1)}, f32[8,32,128]{2,1,0:T(8,128)S(1)}, u32[]{:S(2)}, u32[]{:S(2)}) collective-permute-start(f32[8,32,128]{2,1,0:T(8,128)S(1)} %get-tuple-element.5), channel_id=1, source_target_pairs={{1,0},{2,1},{3,2},{4,3},{5,4},{6,5},{7,6},{0,7},{9,8},{10,9},{11,1... | collective-permute-start | bytes 393224 | tf_op jit(solution)/shard_map/ppermute | solution.py:234

commit v9 on v6

--- a/solution.py
+++ b/solution.py
@@ -60,7 +60,7 @@
     top = sub < 4
     own = (sub < 2) | (sub >= 6)
 
-    @pl.loop(0, 4)
+    @pl.loop(0, 4, unroll=4)
     def _(c):
         for d in range(16):
             lo, hi = SEND[(d + 15) % 16], SEND[(d + 1) % 16]

time: 59.2 us -> 59 us (level)
  no operation moved by 1% of the time
where the time goes in v9:
time: 59 us; the launch traced here: 58.8 us
  blocking collectives  23.3 us (39%)
  starting transfers between devices  18.4 us (31%)
  waiting for transfers between devices  11.4 us (19%)
  Pallas kernels  5.08 us (9%)
  between operations  0.68 us (1%)
    all_to_all x1, blocking collectives, local(): lax.all_to_all(send, 'gx', 0, 0, tiled=True, axis_index_groups=[BACK])  23.3 us
    all_to_all x1, waiting for transfers between devices, local(): lax.all_to_all(pieces, 'gx', 0, 0, tiled=True, axis_index_groups=[ORDER])  10.9 us
    all_to_all x1, starting transfers between devices, local(): lax.all_to_all(pieces, 'gx', 0, 0, tiled=True, axis_index_groups=[ORDER])  8.65 us
    ppermute x1, starting transfers between devices, local(): partner = lax.ppermute(cells, 'gy', [(0, 1), (1, 0)])  4.18 us
    ppermute x1, starting transfers between devices, local(): hi = lax.ppermute(lower, 'gz', down)  3.93 us
    pallas_call x1, Pallas kernels, local(): pl.pallas_call(inner_kernel, out_shape=block, in_specs=[VMEM] * 2, out_sp...  3.36 us
    ppermute x1, starting transfers between devices, local(): lo = lax.ppermute(upper, 'gz', up)  1.64 us
  transfers between devices with their start and end apart: 4, of which 2 were waited for; matrix products, arithmetic and copies ran while one was open for 0% of the time, Pallas kernels for 6%

profile of v9, /device:TPU:1, one launch (start us, length us, event | category | flops | bytes accessed | tf_op | source)
XLA Modules:
  0.0 58.8 jit_solution(11592484489881914038)
XLA Ops:
  0.0 0.0 copy-start.1
  0.0 0.0 copy-start
  0.0 8.7 %all-to-all-start = ((f32[16,8,16,128]{3,2,1,0:T(8,128)}), f32[16,8,16,128]{3,2,1,0:T(8,128)S(1)}, u32[]{:S(2)}, u32[]{:S(2)}) async-start(f32[16,8,16,128]{3,2,1,0:T(8,128)} %bitcast.1), calls=%async_computation | async-start | bytes 2097152 | tf_op jit(solution)/shard_map/all_to_all | solution.py:228
  9.3 10.9 %all-to-all-done.src_ref = f32[16,8,16,128]{3,2,1,0:T(8,128)S(1)} async-done(((f32[16,8,16,128]{3,2,1,0:T(8,128)}), f32[16,8,16,128]{3,2,1,0:T(8,128)S(1)}, u32[]{:S(2)}, u32[]{:S(2)}) %all-to-all-start) | async-done | bytes 1048608 | tf_op jit(solution)/shard_map/all_to_all | solution.py:228
  20.3 0.0 copy-done.1
  20.3 0.0 copy-done
  20.3 0.5 shift.1
  20.8 23.3 %all_to_all.10.src_ref = f32[16,192,128]{2,1,0:T(8,128)S(1)} all-to-all(f32[16,192,128]{2,1,0:T(8,128)S(1)} %shift.1), channel_id=1, replica_groups={{144,0,32,192,16,240,128,224,160,176,208,112,48,96,80,64},{145,1,33,193..., dimensions={0} | all-to-all | bytes 3145728 | tf_op jit(solution)/shard_map/all_to_all | solution.py:238
  44.1 0.2 sort.1
  44.3 4.2 %collective-permute-start.2 = (f32[16,128,128]{2,1,0:T(8,128)S(1)}, f32[16,128,128]{2,1,0:T(8,128)S(1)}, u32[]{:S(2)}, u32[]{:S(2)}) collective-permute-start(f32[16,128,128]{2,1,0:T(8,128)S(1)} %get-tuple-element.12), channel_id=1, source_target_pairs={{0,8},{8,0},{1,9},{9,1},{2,10},{10,2},{3,11},{11,3},{4,12},{12,4},... | collective-permute-start | bytes 3145736 | tf_op jit(solution)/shard_map/ppermute | solution.py:258
  48.5 1.6 %collective-permute-start = (f32[8,32,128]{2,1,0:T(8,128)S(1)}, f32[8,32,128]{2,1,0:T(8,128)S(1)}, u32[]{:S(2)}, u32[]{:S(2)}) collective-permute-start(f32[8,32,128]{2,1,0:T(8,128)S(1)} %get-tuple-element.10), channel_id=1, source_target_pairs={{0,1},{1,2},{2,3},{3,4},{4,5},{5,6},{6,7},{7,0},{8,9},{9,10},{10,1... | collective-permute-start | bytes 393224 | tf_op jit(solution)/shard_map/ppermute | solution.py:256
  50.1 3.9 %collective-permute-start.1 = (f32[8,32,128]{2,1,0:T(8,128)S(1)}, f32[8,32,128]{2,1,0:T(8,128)S(1)}, u32[]{:S(2)}, u32[]{:S(2)}) collective-permute-start(f32[8,32,128]{2,1,0:T(8,128)S(1)} %get-tuple-element.11), channel_id=1, source_target_pairs={{1,0},{2,1},{3,2},{4,3},{5,4},{6,5},{7,6},{0,7},{9,8},{10,9},{11,1... | collective-permute-start | bytes 393224 | tf_op jit(solution)/shard_map/ppermute | solution.py:257
  54.0 0.0 collective-permute-done.2.p_ref
  54.0 3.4 %inner.1.new_ref = f32[8,16,16,128]{3,2,1,0:T(8,128)S(1)} custom-call(f32[16,192,128]{2,1,0:T(8,128)S(1)} %get-tuple-element.9.t_ref, f32[16,128,128]{2,1,0:T(8,128)S(1)} %collective-permute-done.2.p_ref), custom_call_target="tpu_custom_call" | custom-call | flops 40000000 | bytes 6000000 | tf_op jit(solution)/shard_map/inner/pallas_call | solution.py:260
  57.4 0.4 collective-permute-done.lo_ref
  57.8 0.0 collective-permute-done.1.hi_ref
  57.8 1.0 %edge.1 = f32[8,16,16,128]{3,2,1,0:T(8,128)} custom-call(f32[16,192,128]{2,1,0:T(8,128)S(1)} %get-tuple-element.9.t_ref, f32[8,32,128]{2,1,0:T(8,128)S(1)} %collective-permute-done.lo_ref, f32[8,32,128]{2,1,0:T(8,128)S(1)} %collective-permute-done.1.hi_ref, f32[8,16,16,128]{3,2,1,0:T(8,128)S(1)} %inner.1.new_ref), custom_call_target="tpu_custom_call" | custom-call | tf_op jit(solution)/shard_map/edge/pallas_call | solution.py:275
Async XLA Ops:
  0.0 20.3 %copy-start.1 = (s32[128]{0:T(128)S(1)}, s32[128]{0:T(128)}, u32[]{:S(2)}) copy-start(s32[128]{0:T(128)} %num_ref.1) | copy-start | bytes 1540
  0.0 20.3 %copy-start = (s32[128]{0:T(128)S(1)}, s32[128]{0:T(128)}, u32[]{:S(2)}) copy-start(s32[128]{0:T(128)} %cells_ref.1) | copy-start | bytes 1540
  0.0 20.2 %all-to-all-start = ((f32[16,8,16,128]{3,2,1,0:T(8,128)}), f32[16,8,16,128]{3,2,1,0:T(8,128)S(1)}, u32[]{:S(2)}, u32[]{:S(2)}) async-start(f32[16,8,16,128]{3,2,1,0:T(8,128)} %bitcast.1), calls=%async_computation | async-start | bytes 2097152 | tf_op jit(solution)/shard_map/all_to_all | solution.py:228
  44.3 9.8 %collective-permute-start.2 = (f32[16,128,128]{2,1,0:T(8,128)S(1)}, f32[16,128,128]{2,1,0:T(8,128)S(1)}, u32[]{:S(2)}, u32[]{:S(2)}) collective-permute-start(f32[16,128,128]{2,1,0:T(8,128)S(1)} %get-tuple-element.12), channel_id=1, source_target_pairs={{0,8},{8,0},{1,9},{9,1},{2,10},{10,2},{3,11},{11,3},{4,12},{12,4},... | collective-permute-start | bytes 3145736 | tf_op jit(solution)/shard_map/ppermute | solution.py:258
  48.5 9.3 %collective-permute-start = (f32[8,32,128]{2,1,0:T(8,128)S(1)}, f32[8,32,128]{2,1,0:T(8,128)S(1)}, u32[]{:S(2)}, u32[]{:S(2)}) collective-permute-start(f32[8,32,128]{2,1,0:T(8,128)S(1)} %get-tuple-element.10), channel_id=1, source_target_pairs={{0,1},{1,2},{2,3},{3,4},{4,5},{5,6},{6,7},{7,0},{8,9},{9,10},{10,1... | collective-permute-start | bytes 393224 | tf_op jit(solution)/shard_map/ppermute | solution.py:256
  50.1 7.7 %collective-permute-start.1 = (f32[8,32,128]{2,1,0:T(8,128)S(1)}, f32[8,32,128]{2,1,0:T(8,128)S(1)}, u32[]{:S(2)}, u32[]{:S(2)}) collective-permute-start(f32[8,32,128]{2,1,0:T(8,128)S(1)} %get-tuple-element.11), channel_id=1, source_target_pairs={{1,0},{2,1},{3,2},{4,3},{5,4},{6,5},{7,6},{0,7},{9,8},{10,9},{11,1... | collective-permute-start | bytes 393224 | tf_op jit(solution)/shard_map/ppermute | solution.py:257
